TPU v7x, 32 devices: a whole 2x2x4 slice. The times are simulated.
32 devices in a mesh: section: 4 (over x, core), fsdp: 8 (over z, y).
Axes of the slice: x: 2, y: 2, z: 4, core: 2. Of those that a mesh axis runs over, the one named last changes fastest.
Arguments:
- student_w: bfloat16 [4, 1, 3072, 3072], P('section', None, 'fsdp'), may hold values from -0.109375 to 0.109375
- teacher_w: float32 [4, 1, 3072, 3072], P('section', None, 'fsdp'), may hold values from -0.109375 to 0.109375
- saved_in: bfloat16 [4, 1, 4, 256, 3072], P('section', None, None, 'fsdp'), may hold values from -6 to 6
- saved_pre: bfloat16 [4, 1, 4, 256, 3072], P('section', None, None, 'fsdp'), may hold values from -6 to 6
- cotangent: bfloat16 [4, 256, 3072], P(None, 'fsdp'), may hold values from -6 to 6
- slot_order: int32 [4], replicated, may hold values from 0 to 3, each once
- layer_counts: int32 [4], replicated, may hold values from 0 to 1, as said below
- teacher_in: bfloat16 [2, 256, 3072], P(None, 'fsdp'), may hold values from -6 to 6
Outputs:
- input_grad: bfloat16 [4, 4, 256, 3072], P('section', None, 'fsdp')
- grad_shards: bfloat16 [4, 1, 3072, 3072], P('section', None, 'fsdp')
- teacher_new: float32 [4, 1, 3072, 3072], P('section', None, 'fsdp')
- teacher_out: bfloat16 [4, 2, 256, 3072], P('section', None, 'fsdp')
Inputs may be any that keep to these rules, and one draw needn't show every extreme that they name: `layer_counts`: every section holds 0 to 1 layers; some section holds 1 and some holds none. `slot_order`: each micro-batch appears in exactly one slot.
All inputs are finite; a program needn't handle non-finite values.
Results may differ from a plain program's by a relative error of at most 0.019.
Values may be sent and summed in bfloat16 or wider, within the bound.
No kernel may reach another device: no remote copies, remote signals or barrier semaphores. Data moves between devices by JAX's collectives and lax.ppermute only.
A program may use at most 192 MiB of HBM per device.

v0:
```python
import functools
import math

import jax
import jax.numpy as jnp
from jax import lax
from jax.experimental import pallas as pl
from jax.experimental.pallas import tpu as pltpu
from jax.sharding import PartitionSpec as P

epsilon = 1e-06
momentum = 0.996
f32 = jnp.float32
bf16 = jnp.bfloat16


def swap(block, axis, bits):
    size = lax.axis_size(axis)
    return lax.ppermute(block, axis, [(i, i ^ bits) for i in range(size)])


def reorder(blocks, axis):
    me = lax.axis_index(axis)
    return jnp.stack(
        [lax.dynamic_index_in_dim(blocks, me ^ j, 0, False) for j in range(blocks.shape[0])]
    )


def gather(block, axis):
    return reorder(lax.all_gather(block, axis, axis=0), axis)


def exchange(blocks, axis):
    return lax.all_to_all(blocks, axis, split_axis=0, concat_axis=0, tiled=True)


def exchange_near(blocks, axis):
    return reorder(exchange(reorder(blocks, axis), axis), axis)


def add(a, b):
    return a.astype(f32) + b.astype(f32)


def reduce_near(blocks, axis):
    return jnp.sum(exchange_near(blocks, axis).astype(f32), axis=0)


def scatter_from(root, block_at):
    size = lax.axis_size("section")
    blocks = exchange(jnp.stack([block_at(j) for j in range(size)]), "section")
    return lax.dynamic_index_in_dim(blocks, root, 0, False)


def normalize(values):
    wide = values.astype(f32)
    factor = lax.rsqrt(jnp.mean(wide * wide, axis=-1, keepdims=True) + epsilon)
    return (wide * factor, factor)


def gelu_slope(pre):
    wide = pre.astype(f32)
    return 0.5 * (1.0 + lax.erf(wide / math.sqrt(2.0))) + wide * jnp.exp(
        -0.5 * wide * wide
    ) / math.sqrt(2.0 * math.pi)


def times_slope(incoming, pre):
    return (incoming.astype(f32) * gelu_slope(pre)).astype(bf16)


def on_any_mesh(
    student_w, teacher_w, saved_in, saved_pre, cotangent, slot_order, layer_counts, teacher_in
):
    sections = lax.axis_size("section")
    groups = lax.axis_size("fsdp")
    section_id = lax.axis_index("section")
    slots, tokens, width = cotangent.shape
    student = student_w[0, 0]
    deep, wide = student.shape
    columns = wide // sections
    rows = slots * tokens
    part = rows // sections
    rows_f = teacher_in.shape[0] * tokens
    part_f = rows_f // sections
    inputs_own = saved_in[0, 0].reshape(rows, width)
    pre_own = saved_pre[0, 0].reshape(rows, wide)
    scale = 1.0 / math.sqrt(rows * groups)

    active = layer_counts > 0
    flags = active.astype(jnp.int32)
    total = jnp.sum(flags)
    up_to = jnp.cumsum(flags)
    ids = jnp.arange(sections)

    def met(place):
        back = jnp.sum(jnp.where(active & (total - up_to == place), ids, 0))
        ahead = jnp.sum(jnp.where(active & (up_to - 1 == place), ids, 0))
        return back, ahead

    done_back = jnp.sum(jnp.where(ids >= section_id, flags, 0))
    done_ahead = jnp.sum(jnp.where(ids <= section_id, flags, 0))

    teacher_new = momentum * teacher_w[0, 0] + (1.0 - momentum) * student.astype(f32)
    teacher_low = teacher_new.astype(bf16)

    def column_block(array):
        return lambda j: lax.dynamic_slice_in_dim(array, j * columns, columns, 1)

    def row_block(array, count):
        return lambda j: lax.dynamic_slice_in_dim(array, j * count, count, 0)

    def to_features(values):
        blocks = values.reshape(values.shape[0], groups, deep).transpose(1, 0, 2)
        return reorder(exchange(blocks, "fsdp"), "fsdp")

    def stage(place, grad, hidden, slopes):
        back, ahead = met(place)
        normed_h, _ = normalize(hidden)
        feats_h = gather(to_features(normed_h.astype(bf16)), "section")
        teacher = scatter_from(ahead, column_block(teacher_low))
        pre = jnp.dot(
            feats_h.reshape(-1, deep), teacher, preferred_element_type=f32
        ).astype(bf16)
        pre = pre.reshape(sections, groups, part_f, columns).transpose(1, 0, 2, 3)
        pre = reduce_near(pre, "fsdp").astype(bf16)
        pre = reorder(exchange_near(pre, "section"), "section")
        pre = pre.transpose(1, 0, 2).reshape(part_f, wide).astype(f32)
        hidden = (hidden.astype(f32) + jax.nn.gelu(pre, approximate=False)).astype(bf16)
        inputs = scatter_from(back, row_block(inputs_own, part))
        weight = scatter_from(back, column_block(student))
        slopes = gather(slopes, "fsdp").reshape(-1, columns)
        dn = lax.dot_general(
            slopes, weight, (((1,), (1,)), ((), ())), preferred_element_type=f32
        ).astype(bf16)
        dn = dn.reshape(groups, sections, part, deep).transpose(1, 0, 2, 3)
        dn = reduce_near(dn, "section").astype(bf16)
        dn = exchange(reorder(dn, "fsdp"), "fsdp")
        dn = dn.transpose(1, 0, 2).reshape(part, width).astype(f32)
        normed, factor = normalize(inputs)
        grad = (
            grad.astype(f32)
            + factor * (dn - normed * jnp.mean(dn * normed, axis=-1, keepdims=True))
        ).astype(bf16)
        feats = gather(to_features(normed.astype(bf16)), "section").transpose(1, 0, 2, 3)
        term = lax.dot_general(
            feats.reshape(-1, deep), slopes, (((0,), (0,)), ((), ())), preferred_element_type=f32
        )
        term = reorder(gather((scale * term).astype(bf16), "section"), "section")
        return grad, hidden, term.transpose(1, 0, 2).reshape(deep, wide), back

    def publish(grad, hidden):
        both = reorder(gather(jnp.concatenate([grad, hidden]), "section"), "section")
        return both[:, :part].reshape(rows, width), both[:, part:].reshape(rows_f, width)

    cot = jnp.stack([cotangent[slot_order[k]] for k in range(slots)]).reshape(rows, width)
    fed = teacher_in.reshape(rows_f, width)
    grad = row_block(cot, part)(section_id)
    hidden = row_block(fed, part_f)(section_id)
    slopes = scatter_from(met(0)[0], column_block(times_slope(cot, pre_own)))
    slopes = reorder(slopes.reshape(sections, part, columns), "section")
    grad, hidden, term, back = stage(0, grad, hidden, slopes)
    weight_grad = jnp.where(section_id == back, term, jnp.zeros_like(term))

    def next_stage(place, operands):
        grad, hidden, out_grad, out_hidden, weight_grad = operands
        seen_grad, seen_hidden = publish(grad, hidden)
        out_grad = jnp.where(done_back == place, seen_grad, out_grad)
        out_hidden = jnp.where(done_ahead == place, seen_hidden, out_hidden)
        pre = scatter_from(met(place)[0], row_block(pre_own, part))
        slopes = times_slope(grad, pre).reshape(part, sections, columns).transpose(1, 0, 2)
        slopes = exchange_near(reorder(slopes, "section"), "section")
        grad, hidden, term, back = stage(place, grad, hidden, slopes)
        weight_grad = jnp.where(section_id == back, term, weight_grad)
        return grad, hidden, out_grad, out_hidden, weight_grad

    carry = (grad, hidden, cot, fed, weight_grad)
    for place in range(1, sections - 1):
        carry = lax.cond(
            place < total, lambda c, place=place: next_stage(place, c), lambda c: c, carry
        )
    grad, hidden, out_grad, out_hidden, weight_grad = carry
    seen_grad, seen_hidden = publish(grad, hidden)
    out_grad = jnp.where(done_back == total, seen_grad, out_grad)
    out_hidden = jnp.where(done_ahead == total, seen_hidden, out_hidden)
    return (
        out_grad.reshape((1,) + cotangent.shape),
        weight_grad[None, None],
        teacher_new[None, None],
        out_hidden.reshape((1,) + teacher_in.shape),
    )


vmem = pl.BlockSpec(memory_space=pltpu.VMEM)
smem = pl.BlockSpec(memory_space=pltpu.SMEM)
anywhere = pl.BlockSpec(memory_space=pl.ANY)
in_hbm = pl.BlockSpec(memory_space=pltpu.HBM)
params = pltpu.CompilerParams(vmem_limit_bytes=40 * 2**20)


def call(body, name, operands, spaces, out_shape, out_spaces, **more):
    return pl.pallas_call(
        body,
        in_specs=spaces,
        out_specs=out_spaces,
        out_shape=out_shape,
        compiler_params=params,
        name=name,
        **more,
    )(*operands)


def shaped(shape, dtype=bf16):
    return jax.ShapeDtypeStruct(shape, dtype)


def window(block, size):
    return pl.ds(pl.multiple_of(block * size, size), size)


class Plan:
    def __init__(self, sections):
        self.section, self.group, self.total, self.back = 0, 1, 2, 3
        self.ahead = self.back + sections + 1
        self.done_back = self.ahead + sections + 1
        self.done_ahead = self.done_back + sections
        self.size = self.done_ahead + sections


def plan_kernel(where, counts_ref, section_ref, group_ref, out_ref):
    sections = counts_ref.shape[0]
    out_ref[where.section] = section_ref[0]
    out_ref[where.group] = group_ref[0]
    seen = jnp.int32(0)
    for s in range(sections):
        out_ref[where.ahead + seen] = jnp.int32(s)
        seen = seen + (counts_ref[s] > 0).astype(jnp.int32)
        out_ref[where.done_ahead + s] = seen
    out_ref[where.total] = seen
    out_ref[where.ahead + sections] = jnp.int32(0)
    seen = jnp.int32(0)
    for s in reversed(range(sections)):
        out_ref[where.back + seen] = jnp.int32(s)
        seen = seen + (counts_ref[s] > 0).astype(jnp.int32)
        out_ref[where.done_back + s] = seen
    out_ref[where.back + sections] = jnp.int32(0)


def make_plan(where, counts):
    me = [lax.axis_index(axis).astype(jnp.int32)[None] for axis in ("section", "fsdp")]
    return call(
        functools.partial(plan_kernel, where),
        "make_plan",
        (counts, *me),
        [smem] * 3,
        shaped((where.size,), jnp.int32),
        smem,
    )


def first_kernel(where, plan, order, cot, pre, near_out, far_out, grad_out):
    sections, _, columns = near_out.shape[1:]
    me = plan[where.section]
    grad_out[...] = cot[order[me]]
    for distance in range(sections):
        target = me ^ distance
        out = (near_out, far_out)[distance & 1]
        for slot in range(sections):
            out[distance >> 1, pl.ds(slot ^ target, 1)] = times_slope(
                cot[order[slot], :, window(target, columns)],
                pre[slot, :, window(target, columns)],
            )[None]


def first_slopes(where, plan, order, cot, pre):
    sections, part, wide = pre.shape
    half = shaped((sections // 2, sections, part, wide // sections))
    return call(
        functools.partial(first_kernel, where),
        "first_slopes",
        (plan, order, cot, pre),
        [smem, smem, vmem, vmem],
        [half, half, shaped((part, wide))],
        [vmem] * 3,
    )


def weights_kernel(where, plan, student_ref, teacher_ref, new_ref, s_near, s_far, t_near, t_far):
    sections, columns = 2 * s_near.shape[0], s_near.shape[2]
    new_ref[...] = momentum * teacher_ref[...] + (1.0 - momentum) * student_ref[...].astype(f32)
    for distance in range(sections):
        cols = window(plan[where.section] ^ distance, columns)
        (s_near, s_far)[distance & 1][distance >> 1] = student_ref[:, cols]
        (t_near, t_far)[distance & 1][distance >> 1] = new_ref[:, cols].astype(bf16)


def split_weights(where, plan, student, teacher, sections):
    deep, wide = student.shape
    tile = 64
    columns = wide // sections
    whole = pl.BlockSpec((tile, wide), lambda i: (i, 0))
    half = pl.BlockSpec((sections // 2, tile, columns), lambda i: (0, i, 0))
    out = shaped((sections // 2, deep, columns))
    return call(
        functools.partial(weights_kernel, where),
        "split_weights",
        (plan, student, teacher),
        [smem, whole, whole],
        [shaped(teacher.shape, f32)] + [out] * 4,
        [whole] + [half] * 4,
        grid=(deep // tile,),
    )


def rows_kernel(where, plan, inputs_ref, pre_ref, near_out, far_out):
    part = inputs_ref.shape[1]
    for distance in range(inputs_ref.shape[0]):
        target = plan[where.section] ^ distance
        out = (near_out, far_out)[distance & 1]
        out[distance >> 1, :part] = inputs_ref[target]
        out[distance >> 1, part:] = pre_ref[target]


def split_rows(where, plan, inputs, pre):
    sections, part, wide = inputs.shape
    half = shaped((sections // 2, 2 * part, wide))
    return call(
        functools.partial(rows_kernel, where),
        "split_rows",
        (plan, inputs, pre),
        [smem, vmem, vmem],
        [half, half],
        [vmem] * 2,
    )


def send_kernel(where, root_at, plan, place, *refs):
    count = len(root_at)
    outs, sem = refs[2 * count : 3 * count], refs[3 * count]
    for i, at in enumerate(root_at):
        distance = plan[where.section] ^ plan[at + place[0]]
        for core in (0, 1):

            @pl.when((distance & 1) == core)
            def _(i=i, core=core):
                pltpu.make_async_copy(refs[2 * i + core].at[1], outs[i], sem.at[i]).start()

    for i in range(count):
        pltpu.make_async_copy(refs[2 * i].at[1], outs[i], sem.at[i]).wait()


def sends(where, plan, place, roots, pairs):
    flat = [half for pair in pairs for half in pair]
    return call(
        functools.partial(send_kernel, where, tuple(roots)),
        "send_blocks",
        (plan, place, *flat),
        [smem, smem] + [anywhere] * len(flat),
        [shaped(near.shape[1:]) for near, _ in pairs],
        [vmem] * len(pairs),
        scratch_shapes=[pltpu.SemaphoreType.DMA((len(pairs),))],
    )


def across(where, plan, place, roots, pairs):
    return [swap(block, "section", 2) for block in sends(where, plan, place, roots, pairs)]


def fetch(distance, near, far, came, held, sem):
    choices = ((near.at[0], 0), (far.at[0], 1), (came, 2), (came, 3))
    for source, at in choices:

        @pl.when(distance == at)
        def _(source=source):
            pltpu.make_async_copy(source, held, sem).start()

    pltpu.make_async_copy(came, held, sem).wait()


def take_kernel(where, plan, place, near, far, came, inputs_out, pre_out, sem):
    distance = plan[where.section] ^ plan[where.back + place[0]]
    part = inputs_out.shape[0]
    for j, out in enumerate((inputs_out, pre_out)):
        rows = pl.ds(j * part, part)
        for source, at in ((near.at[0], 0), (far.at[0], 1), (came, 2), (came, 3)):

            @pl.when(distance == at)
            def _(source=source, out=out, rows=rows, j=j):
                pltpu.make_async_copy(source.at[rows], out, sem.at[j]).start()

    for j, out in enumerate((inputs_out, pre_out)):
        pltpu.make_async_copy(came.at[pl.ds(j * part, part)], out, sem.at[j]).wait()


def take_rows(where, plan, place, near, far, came):
    part = came.shape[0] // 2
    return call(
        functools.partial(take_kernel, where),
        "take_rows",
        (plan, place, near, far, came),
        [smem, smem] + [anywhere] * 3,
        [shaped((part, came.shape[1]))] * 2,
        [vmem] * 2,
        scratch_shapes=[pltpu.SemaphoreType.DMA((2,))],
    )


def choose_kernel(where, plan, near, far, came, out, sem):
    distance = plan[where.section] ^ plan[where.back]
    fetch(distance, near, far, came, out, sem)


def choose(where, plan, near, far, came):
    return call(
        functools.partial(choose_kernel, where),
        "choose",
        (plan, near, far, came),
        [smem] + [anywhere] * 3,
        shaped(came.shape),
        vmem,
        scratch_shapes=[pltpu.SemaphoreType.DMA],
    )


def features_kernel(inputs_ref, hidden_ref, out_ref):
    groups, _, deep = out_ref.shape
    part = inputs_ref.shape[0]
    for rows, ref in ((pl.ds(0, part), inputs_ref), (pl.ds(part, hidden_ref.shape[0]), hidden_ref)):
        normed = normalize(ref[...])[0].astype(bf16)
        for j in range(groups):
            out_ref[j, rows] = normed[:, j * deep : (j + 1) * deep]


def features(inputs, hidden, groups):
    rows = inputs.shape[0] + hidden.shape[0]
    return call(
        features_kernel,
        "features",
        (inputs, hidden),
        [vmem, vmem],
        shaped((groups, rows, inputs.shape[1] // groups)),
        vmem,
    )


def back_kernel(where, plan, place, slopes_ref, near, far, came, stay_out, go_out, weight, sem):
    groups, sections, part, columns = slopes_ref.shape
    distance = plan[where.section] ^ plan[where.back + place[0]]
    fetch(distance, near, far, came, weight, sem)
    for k in range(groups):
        dn = lax.dot_general(
            slopes_ref[k].reshape(sections * part, columns),
            weight[...],
            (((1,), (1,)), ((), ())),
            preferred_element_type=f32,
        ).astype(bf16)
        dn = dn.reshape(sections, part, weight.shape[0])
        for s in range(sections):
            out = (stay_out, go_out)[s & 1]
            out[s >> 1, pl.ds(plan[where.group] ^ k, 1)] = dn[s][None]


def back_product(where, plan, place, slopes, near, far, came):
    groups, sections, part, _ = slopes.shape
    out = shaped((sections // 2, groups, part, came.shape[0]))
    return call(
        functools.partial(back_kernel, where),
        "back_product",
        (plan, place, slopes, near, far, came),
        [smem, smem, vmem] + [anywhere] * 3,
        [out, out],
        [vmem] * 2,
        scratch_shapes=[pltpu.VMEM(came.shape, bf16), pltpu.SemaphoreType.DMA],
    )


def ahead_kernel(where, part, plan, place, feats_ref, near, far, came, stay_out, go_out, weight, sem):
    sections, groups, rows, deep = feats_ref.shape
    part_f, columns = rows - part, came.shape[1]
    distance = plan[where.section] ^ plan[where.ahead + place[0]]
    fetch(distance, near, far, came, weight, sem)
    side = plan[where.group] & 1
    for s in range(sections):
        pre = jnp.dot(
            feats_ref[s, :, part:, :].reshape(groups * part_f, deep),
            weight[...],
            preferred_element_type=f32,
        ).astype(bf16)
        pre = pre.reshape(groups, part_f, columns)
        for j in range(0, groups, 2):
            seat = (plan[where.group] ^ j) >> 1
            stay_out[pl.ds(seat, 1), s] = jnp.where(side == 0, pre[j], pre[j + 1])[None]
            go_out[pl.ds(seat, 1), s] = jnp.where(side == 0, pre[j + 1], pre[j])[None]


def ahead_product(where, part, plan, place, feats, near, far, came):
    sections, groups, rows, _ = feats.shape
    out = shaped((groups // 2, sections, rows - part, came.shape[1]))
    return call(
        functools.partial(ahead_kernel, where, part),
        "ahead_product",
        (plan, place, feats, near, far, came),
        [smem, smem, vmem] + [anywhere] * 3,
        [out, out],
        [vmem] * 2,
        scratch_shapes=[pltpu.VMEM(came.shape, bf16), pltpu.SemaphoreType.DMA],
    )


def grad_kernel(where, scale, plan, feats_ref, slopes_ref, out_ref, total_ref):
    groups, sections, part, columns = slopes_ref.shape
    deep = feats_ref.shape[3]
    for k in range(groups):
        feats = feats_ref[:, pl.ds(plan[where.group] ^ k, 1), :part, :]
        term = lax.dot_general(
            feats.reshape(sections * part, deep),
            slopes_ref[k].reshape(sections * part, columns),
            (((0,), (0,)), ((), ())),
            preferred_element_type=f32,
        )
        if k == 0:
            total_ref[...] = term
        else:
            total_ref[...] += term
    out_ref[...] = (scale * total_ref[...]).astype(bf16)


def grad_product(where, scale, plan, feats, slopes):
    size = (feats.shape[3], slopes.shape[3])
    return call(
        functools.partial(grad_kernel, where, scale),
        "grad_product",
        (plan, feats, slopes),
        [smem, vmem, vmem],
        shaped(size),
        vmem,
        scratch_shapes=[pltpu.VMEM(size, f32)],
    )


def slopes_kernel(where, plan, grad_ref, pre_ref, out_ref):
    sections, _, columns = out_ref.shape
    for distance in range(sections):
        cols = window(plan[where.section] ^ distance, columns)
        out_ref[distance] = times_slope(grad_ref[:, cols], pre_ref[:, cols])


def slope_blocks(where, plan, grad, pre, sections):
    part, wide = pre.shape
    return call(
        functools.partial(slopes_kernel, where),
        "slope_blocks",
        (plan, grad, pre),
        [smem, vmem, vmem],
        shaped((sections, part, wide // sections)),
        vmem,
    )


def write_seen(done, sections, plan, place, values, outs, sem):
    for start in (True, False):
        for s in range(sections):

            @pl.when(plan[done + s] == place[0] + 1)
            def _(s=s, start=start):
                copy = pltpu.make_async_copy(values, outs.at[s], sem.at[s])
                copy.start() if start else copy.wait()


def update_kernel(where, plan, place, grad_ref, inputs_ref, dn_ref, old, out_ref, outs, sem):
    groups = dn_ref.shape[0]
    dn = jnp.concatenate([dn_ref[j].astype(f32) for j in range(groups)], axis=1)
    normed, factor = normalize(inputs_ref[...])
    grad = grad_ref[...].astype(f32) + factor * (
        dn - normed * jnp.mean(dn * normed, axis=-1, keepdims=True)
    )
    out_ref[...] = grad.astype(bf16)
    write_seen(where.done_back, old.shape[0], plan, place, out_ref, outs, sem)


def update(where, plan, place, grad, inputs, dn, outs):
    return call(
        functools.partial(update_kernel, where),
        "update",
        (plan, place, grad, inputs, dn, outs),
        [smem, smem, vmem, vmem, vmem, anywhere],
        [shaped(grad.shape), shaped(outs.shape)],
        [vmem, anywhere],
        scratch_shapes=[pltpu.SemaphoreType.DMA((outs.shape[0],))],
        input_output_aliases={5: 1},
    )


def hidden_kernel(where, plan, place, hidden_ref, pre_ref, old, out_ref, outs, sem):
    sections, _, columns = pre_ref.shape
    for distance in range(sections):
        cols = window(plan[where.section] ^ distance, columns)
        pre = pre_ref[distance].astype(f32)
        gelu = 0.5 * pre * (1.0 + lax.erf(pre / math.sqrt(2.0)))
        out_ref[:, cols] = (hidden_ref[:, cols].astype(f32) + gelu).astype(bf16)
    write_seen(where.done_ahead, old.shape[0], plan, place, out_ref, outs, sem)


def update_hidden(where, plan, place, hidden, pre, outs):
    return call(
        functools.partial(hidden_kernel, where),
        "update_hidden",
        (plan, place, hidden, pre, outs),
        [smem, smem, vmem, vmem, anywhere],
        [shaped(hidden.shape), shaped(outs.shape)],
        [vmem, anywhere],
        scratch_shapes=[pltpu.SemaphoreType.DMA((outs.shape[0],))],
        input_output_aliases={4: 1},
    )


def store_kernel(where, plan, place, *refs):
    terms, out, sem = refs[:4], refs[5], refs[6]
    columns = terms[0].shape[1]

    @pl.when(plan[where.section] == plan[where.back + place[0]])
    def _():
        copies = [
            pltpu.make_async_copy(
                term, out.at[:, window(plan[where.section] ^ distance, columns)], sem.at[distance]
            )
            for distance, term in enumerate(terms)
        ]
        for copy in copies:
            copy.start()
        for copy in copies:
            copy.wait()


def store(where, plan, place, terms, old):
    return call(
        functools.partial(store_kernel, where),
        "store",
        (plan, place, *terms, old),
        [smem, smem] + [anywhere] * 5,
        shaped(old.shape),
        anywhere,
        scratch_shapes=[pltpu.SemaphoreType.DMA((4,))],
        input_output_aliases={6: 0},
    )


def pack_kernel(where, plan, grads, hiddens, *refs):
    outs, sem = refs[:-1], refs[-1]
    part = grads.shape[1]
    for wait in (False, True):
        for distance, out in enumerate(outs):
            target = plan[where.section] ^ distance
            for j, (source, rows) in enumerate(
                ((grads, pl.ds(0, part)), (hiddens, pl.ds(part, hiddens.shape[1])))
            ):
                copy = pltpu.make_async_copy(source.at[target], out.at[rows], sem.at[2 * distance + j])
                copy.wait() if wait else copy.start()


def pack(where, plan, grads, hiddens):
    sections, part, width = grads.shape
    out = shaped((part + hiddens.shape[1], width))
    return call(
        functools.partial(pack_kernel, where),
        "pack",
        (plan, grads, hiddens),
        [smem, anywhere, anywhere],
        [out] * sections,
        [vmem] * sections,
        scratch_shapes=[pltpu.SemaphoreType.DMA((2 * sections,))],
    )


def unpack_kernel(where, plan, *refs):
    pieces, (grads, hiddens, sem) = refs[:-3], refs[-3:]
    part = grads.shape[1]
    for wait in (False, True):
        for distance, piece in enumerate(pieces):
            source = plan[where.section] ^ distance
            for j, (out, rows) in enumerate(
                ((grads, pl.ds(0, part)), (hiddens, pl.ds(part, hiddens.shape[1])))
            ):
                copy = pltpu.make_async_copy(piece.at[rows], out.at[source], sem.at[2 * distance + j])
                copy.wait() if wait else copy.start()


def unpack(where, plan, pieces, part):
    rows, width = pieces[0].shape
    return call(
        functools.partial(unpack_kernel, where),
        "unpack",
        (plan, *pieces),
        [smem] + [anywhere] * len(pieces),
        [shaped((len(pieces), part, width)), shaped((len(pieces), rows - part, width))],
        [in_hbm] * 2,
        scratch_shapes=[pltpu.SemaphoreType.DMA((2 * len(pieces),))],
    )


def from_sections(block):
    beside = swap(block, "section", 1)
    over = swap(block, "section", 2)
    return [block, beside, over, swap(over, "section", 1)]


def to_sections(blocks):
    return jnp.stack([blocks[0]] + [swap(blocks[k], "section", k) for k in (1, 2, 3)])


def from_groups(block):
    line = [block] + [swap(block, "fsdp", bits) for bits in (2, 4, 6)]
    other = [swap(b, "fsdp", 1) for b in line]
    return jnp.stack([b for pair in zip(line, other) for b in pair])


def sum_halves(stay, go, axis):
    near = add(stay, swap(go, axis, 1)).astype(bf16)
    total = near[0].astype(f32)
    for k in range(1, near.shape[0]):
        total = total + swap(near[k], axis, 2 * k).astype(f32)
    return total.astype(bf16)


def fence(*values):
    return lax.optimization_barrier(values)


def on_four_by_eight(
    student_w, teacher_w, saved_in, saved_pre, cotangent, slot_order, layer_counts, teacher_in
):
    sections = lax.axis_size("section")
    groups = lax.axis_size("fsdp")
    slots, tokens, width = cotangent.shape
    student = student_w[0, 0]
    deep, wide = student.shape
    rows = slots * tokens
    part = rows // sections
    part_f = teacher_in.shape[0] * tokens // sections
    scale = 1.0 / math.sqrt(rows * groups)
    where = Plan(sections)
    plan = make_plan(where, layer_counts)
    inputs_own = saved_in[0, 0].reshape(sections, part, width)
    pre_own = saved_pre[0, 0].reshape(sections, part, wide)

    def to_groups(blocks):
        return lax.all_to_all(blocks, "fsdp", 0, 0, tiled=True)

    def stage(place, grad, hidden, slopes, inputs, outs, spreads, first=False):
        weight, low, saved = spreads
        outs_grad, outs_hidden, weight_grad = outs
        if first:
            feats = to_groups(features(inputs, hidden, groups))
            feats, slopes = fence(feats, slopes)
            came = across(where, plan, place, (where.ahead, where.back), (low, weight))
            slopes = from_groups(slopes)
        else:
            came = across(where, plan, place, (where.ahead, where.back), (low, weight))
            line = [slopes] + [swap(slopes, "fsdp", bits) for bits in (2, 4, 6)]
            line[1], line[3], inputs, hidden = fence(line[1], line[3], inputs, hidden)
            feats = to_groups(features(inputs, hidden, groups))
            slopes = jnp.stack([b for near in line for b in (near, swap(near, "fsdp", 1))])
        low_came, weight_came = came
        feats = jnp.stack(from_sections(feats))
        pre = ahead_product(where, part, plan, place, feats, *low, low_came)
        pre = to_sections(sum_halves(*pre, "fsdp"))
        hidden, outs_hidden = update_hidden(where, plan, place, hidden, pre, outs_hidden)
        dn = back_product(where, plan, place, slopes, *weight, weight_came)
        dn = lax.all_to_all(sum_halves(*dn, "section"), "fsdp", 0, 0, tiled=True)
        grad, outs_grad = update(where, plan, place, grad, inputs, dn, outs_grad)
        terms = from_sections(grad_product(where, scale, plan, feats, slopes))
        weight_grad = store(where, plan, place, terms, weight_grad)
        (came,) = across(where, plan, place + 1, (where.back,), (saved,))
        inputs, pre = take_rows(where, plan, place + 1, *saved, came)
        return grad, hidden, inputs, pre, (outs_grad, outs_hidden, weight_grad)

    first = jnp.zeros((1,), jnp.int32)
    near, far, grad = first_slopes(where, plan, slot_order, cotangent, pre_own)
    far = swap(far, "section", 1)
    (came,) = across(where, plan, first, (where.back,), ((near, far),))
    slopes = choose(where, plan, near, far, came)
    hidden = lax.dynamic_slice(
        teacher_in.reshape(-1, width),
        (lax.axis_index("section") * part_f, 0),
        (part_f, width),
        allow_negative_indices=False,
    )
    near, far = split_rows(where, plan, inputs_own, pre_own)
    saved = (near, swap(far, "section", 1))
    (came,) = across(where, plan, first, (where.back,), (saved,))
    inputs, _ = take_rows(where, plan, first, *saved, came)
    teacher_new, s_near, s_far, t_near, t_far = split_weights(
        where, plan, student, teacher_w[0, 0], sections
    )
    spreads = ((s_near, swap(s_far, "section", 1)), (t_near, swap(t_far, "section", 1)), saved)
    outs = (
        jnp.broadcast_to(grad, (sections,) + grad.shape),
        jnp.broadcast_to(hidden, (sections,) + hidden.shape),
        jnp.zeros((deep, wide), bf16),
    )
    grad, hidden, inputs, pre, outs = stage(
        first, grad, hidden, slopes, inputs, outs, spreads, True
    )

    def next_stage(carry):
        place, grad, hidden, inputs, pre, outs = carry
        slopes = to_sections(slope_blocks(where, plan, grad, pre, sections))
        grad, hidden, inputs, pre, outs = stage(
            place[None], grad, hidden, slopes, inputs, outs, spreads
        )
        return place + 1, grad, hidden, inputs, pre, outs

    total = plan[where.total]
    carry = (jnp.int32(1), grad, hidden, inputs, pre, outs)
    outs = lax.while_loop(lambda c: c[0] < total, next_stage, carry)[-1]
    blocks = pack(where, plan, *outs[:2])
    pieces = [blocks[0]] + [swap(blocks[k], "section", k) for k in (1, 2, 3)]
    input_grad, teacher_out = unpack(where, plan, pieces, part)
    return (
        input_grad.reshape((1,) + cotangent.shape),
        outs[2][None, None],
        teacher_new[None, None],
        teacher_out.reshape((1,) + teacher_in.shape),
    )


def solution(mesh):
    in_specs = (
        P("section", None, "fsdp", None),
        P("section", None, "fsdp", None),
        P("section", None, None, "fsdp", None),
        P("section", None, None, "fsdp", None),
        P(None, "fsdp", None),
        P(),
        P(),
        P(None, "fsdp", None),
    )
    out_specs = (
        P("section", None, "fsdp", None),
        P("section", None, "fsdp", None),
        P("section", None, "fsdp", None),
        P("section", None, "fsdp", None),
    )
    sizes = dict(mesh.shape)
    fits = sizes["section"] == 4 and sizes["fsdp"] == 8
    return jax.shard_map(
        on_four_by_eight if fits else on_any_mesh, mesh=mesh, in_specs=in_specs, out_specs=out_specs, check_vma=False
    )
```

profile of v0, /device:TPU:0, one launch (start us, length us, event | category | flops | bytes accessed | tf_op | source)
XLA Modules:
  0.0 246.7 jit_solution(4090574941286243316)
XLA Ops:
  6.0 2.3 copy-done.2
  10.0 5.1 %split_weights.1 = (f32[384,3072]{1,0:T(8,128)}, bf16[2,384,768]{2,1,0:T(8,128)(2,1)}, bf16[2,384,768]{2,1,0:T(8,128)(2,1)}, bf16[2,384,768]{2,1,0:T(8,128)(2,1)}, bf16[2,384,768]{2,1,0:T(8,128)(2,1)}) custom-call(s32[21]{0:T(128)S(1)} %make_plan.1.plan, bf16[384,3072]{1,0:T(8,128)(2,1)S(1)} %bitcast.166, f32[384,3072]{1,0:T(8,128)S(1)} %bitcast.163), custom_call_target="tpu_custom_call" | custom-call | tf_op jit(solution)/shard_map/split_weights/pallas_call | solution.py:202
  16.5 2.7 %collective-permute-start.29 = (bf16[64,3072]{1,0:T(8,128)(2,1)S(1)}, bf16[64,3072]{1,0:T(8,128)(2,1)S(1)}, u32[]{:S(2)}, u32[]{:S(2)}) collective-permute-start(bf16[64,3072]{1,0:T(8,128)(2,1)S(1)} %send_blocks.6), channel_id=1, source_target_pairs={{0,16},{8,24},{16,0},{24,8},{1,17},{9,25},{17,1},{25,9},{2,18},{10... | collective-permute-start | bytes 1179656 | tf_op jit(solution)/shard_map/ppermute | solution.py:19
  20.7 8.1 %collective-permute-done.29.came = bf16[64,3072]{1,0:T(8,128)(2,1)S(1)} collective-permute-done((bf16[64,3072]{1,0:T(8,128)(2,1)S(1)}, bf16[64,3072]{1,0:T(8,128)(2,1)S(1)}, u32[]{:S(2)}, u32[]{:S(2)}) %collective-permute-start.29) | collective-permute-done | bytes 393248 | tf_op jit(solution)/shard_map/ppermute | solution.py:19
  31.5 6.1 %all-to-all-start.2 = ((bf16[8,48,384]{2,1,0:T(8,128)(2,1)}), bf16[8,48,384]{2,1,0:T(8,128)(2,1)S(1)}, u32[]{:S(2)}, u32[]{:S(2)}) async-start(bf16[8,48,384]{2,1,0:T(8,128)(2,1)} %features.2), calls=%async_computation.2 | async-start | bytes 589824 | tf_op jit(solution)/shard_map/all_to_all | solution.py:747
  40.0 4.8 %collective-permute-done.31.came = bf16[4,32,768]{2,1,0:T(8,128)(2,1)S(1)} collective-permute-done((bf16[4,32,768]{2,1,0:T(8,128)(2,1)S(1)}, bf16[4,32,768]{2,1,0:T(8,128)(2,1)S(1)}, u32[]{:S(2)}, u32[]{:S(2)}) %collective-permute-start.31) | collective-permute-done | bytes 196640 | tf_op jit(solution)/shard_map/ppermute | solution.py:19
  52.6 2.4 collective-permute-start.35
  55.0 5.2 %collective-permute-done.33 = bf16[4,32,768]{2,1,0:T(8,128)(2,1)S(1)} collective-permute-done((bf16[4,32,768]{2,1,0:T(8,128)(2,1)S(1)}, bf16[4,32,768]{2,1,0:T(8,128)(2,1)S(1)}, u32[]{:S(2)}, u32[]{:S(2)}) %collective-permute-start.33) | collective-permute-done | bytes 196640 | tf_op jit(solution)/shard_map/ppermute | solution.py:19
  60.8 2.8 %collective-permute-start.37 = (bf16[4,32,768]{2,1,0:T(8,128)(2,1)S(1)}, bf16[4,32,768]{2,1,0:T(8,128)(2,1)S(1)}, u32[]{:S(2)}, u32[]{:S(2)}) collective-permute-start(bf16[4,32,768]{2,1,0:T(8,128)(2,1)S(1)} %choose.1), channel_id=1, source_target_pairs={{0,6},{1,7},{2,4},{3,5},{4,2},{5,3},{6,0},{7,1},{8,14},{9,15},{10,... | collective-permute-start | bytes 589832 | tf_op jit(solution)/shard_map/ppermute | solution.py:19
  63.6 2.4 collective-permute-done.35
  72.2 9.2 %collective-permute-done.45 = bf16[8,48,384]{2,1,0:T(8,128)(2,1)S(1)} collective-permute-done((bf16[8,48,384]{2,1,0:T(8,128)(2,1)S(1)}, bf16[8,48,384]{2,1,0:T(8,128)(2,1)S(1)}, u32[]{:S(2)}, u32[]{:S(2)}) %collective-permute-start.45) | collective-permute-done | bytes 294944 | tf_op jit(solution)/shard_map/ppermute | solution.py:19
  89.8 2.7 %collective-permute-start.57 = (bf16[384,768]{1,0:T(8,128)(2,1)S(1)}, bf16[384,768]{1,0:T(8,128)(2,1)S(1)}, u32[]{:S(2)}, u32[]{:S(2)}) collective-permute-start(bf16[384,768]{1,0:T(8,128)(2,1)S(1)} %grad_product.2.refs_0_), channel_id=1, source_target_pairs={{0,16},{8,24},{16,0},{24,8},{1,17},{9,25},{17,1},{25,9},{2,18},{10... | collective-permute-start | bytes 1769480 | tf_op jit(solution)/shard_map/ppermute | solution.py:19
  92.7 7.7 %collective-permute-done.48 = bf16[4,4,16,768]{3,2,1,0:T(8,128)(2,1)S(1)} collective-permute-done((bf16[4,4,16,768]{3,2,1,0:T(8,128)(2,1)S(1)}, bf16[4,4,16,768]{3,2,1,0:T(8,128)(2,1)S(1)}, u32[]{:S(2)}, u32[]{:S(2)}) %collective-permute-start.48) | collective-permute-done | bytes 393248 | tf_op jit(solution)/shard_map/ppermute | solution.py:19
  100.5 3.3 %collective-permute-start.51 = (bf16[4,16,768]{2,1,0:T(8,128)(2,1)S(1)}, bf16[4,16,768]{2,1,0:T(8,128)(2,1)S(1)}, u32[]{:S(2)}, u32[]{:S(2)}) collective-permute-start(bf16[4,16,768]{2,1,0:T(8,128)(2,1)S(1)} %get-tuple-element.214), channel_id=1, source_target_pairs={{0,6},{1,7},{2,4},{3,5},{4,2},{5,3},{6,0},{7,1},{8,14},{9,15},{10,... | collective-permute-start | bytes 294920 | tf_op jit(solution)/shard_map/ppermute | solution.py:19
  105.0 5.0 %collective-permute-done.43 = bf16[8,32,384]{2,1,0:T(8,128)(2,1)S(1)} collective-permute-done((bf16[8,32,384]{2,1,0:T(8,128)(2,1)S(1)}, bf16[8,32,384]{2,1,0:T(8,128)(2,1)S(1)}, u32[]{:S(2)}, u32[]{:S(2)}) %collective-permute-start.43) | collective-permute-done | bytes 196640 | tf_op jit(solution)/shard_map/ppermute | solution.py:19
  113.0 4.6 %all-to-all-start.3 = ((bf16[8,32,384]{2,1,0:T(8,128)(2,1)}), bf16[8,32,384]{2,1,0:T(8,128)(2,1)S(1)}, u32[]{:S(2)}, u32[]{:S(2)}) async-start(bf16[8,32,384]{2,1,0:T(8,128)(2,1)} %fusion.4), calls=%async_computation.3 | async-start | bytes 393216 | tf_op jit(solution)/shard_map/all_to_all | solution.py:769
  121.7 2.3 take_rows.4
  131.5 96.0 %while.22 = (s32[]{:T(128)}, bf16[32,3072]{1,0:T(8,128)(2,1)S(1)}, bf16[16,3072]{1,0:T(8,128)(2,1)}, bf16[32,3072]{1,0:T(8,128)(2,1)}, bf16[32,3072]{1,0:T(8,128...) while((s32[]{:T(128)}, bf16[32,3072]{1,0:T(8,128)(2,1)S(1)}, ...), condition=%wide.region_1.0_spmd, body=%wide.region_0.0_spmd.sunk | while | flops 5357570 | bytes 86411120 | solution.py:815
  141.0 2.4 collective-permute-start.4
  143.9 2.7 %send_blocks.10 = (bf16[384,768]{1,0:T(8,128)(2,1)}, bf16[384,768]{1,0:T(8,128)(2,1)}) custom-call(s32[21]{0:T(128)S(1)} %get-tuple-element.417.plan, s32[1]{0:T(128)} %bitcast.151.place, bf16[2,384,768]{2,1,0:T(8,128)(2,1)} %get-tuple-element.418.refs_0_.near, bf16[2,384,768]{2,1,0:T(8,128)(2,1)} %get-tuple-element.419.refs_1_.far, ...), custom_call_target="tpu_custom_call" | custom-call | tf_op jit(solution)/shard_map/while/body/send_blocks/pallas_call | solution.py:202
  150.0 2.7 %collective-permute-done.4 = bf16[4,32,768]{2,1,0:T(8,128)(2,1)S(1)} collective-permute-done((bf16[4,32,768]{2,1,0:T(8,128)(2,1)}, bf16[4,32,768]{2,1,0:T(8,128)(2,1)S(1)}, u32[]{:S(2)}, u32[]{:S(2)}) %collective-permute-start.4) | collective-permute-done | bytes 196640 | tf_op jit(solution)/shard_map/while/body/ppermute | solution.py:19
  154.5 8.6 %all-to-all-start.1 = ((bf16[8,48,384]{2,1,0:T(8,128)(2,1)}), bf16[8,48,384]{2,1,0:T(8,128)(2,1)}, u32[]{:S(2)}, u32[]{:S(2)}) async-start(bf16[8,48,384]{2,1,0:T(8,128)(2,1)} %features.3), calls=%async_computation.1 | async-start | bytes 589824 | tf_op jit(solution)/shard_map/while/body/all_to_all | solution.py:747
  169.0 2.7 %all-to-all-done.1 = bf16[8,48,384]{2,1,0:T(8,128)(2,1)} async-done(((bf16[8,48,384]{2,1,0:T(8,128)(2,1)}), bf16[8,48,384]{2,1,0:T(8,128)(2,1)}, u32[]{:S(2)}, u32[]{:S(2)}) %all-to-all-start.1) | async-done | bytes 294944 | tf_op jit(solution)/shard_map/while/body/all_to_all | solution.py:747
  174.8 4.9 %collective-permute-done.13 = bf16[8,48,384]{2,1,0:T(8,128)(2,1)S(1)} collective-permute-done((bf16[8,48,384]{2,1,0:T(8,128)(2,1)}, bf16[8,48,384]{2,1,0:T(8,128)(2,1)S(1)}, u32[]{:S(2)}, u32[]{:S(2)}) %collective-permute-start.13) | collective-permute-done | bytes 294944 | tf_op jit(solution)/shard_map/while/body/ppermute | solution.py:19
  179.8 3.0 %back_product.3 = (bf16[2,8,32,384]{3,2,1,0:T(8,128)(2,1)S(1)}, bf16[2,8,32,384]{3,2,1,0:T(8,128)(2,1)S(1)}) custom-call(s32[21]{0:T(128)S(1)} %get-tuple-element.417.plan, s32[1]{0:T(128)} %bitcast.151.place, bf16[8,4,32,768]{3,2,1,0:T(8,128)(2,1)S(1)} %bitcast_dynamic-update-slice_fusion.31.slopes_ref, ...), custom_call_target="tpu_custom_call" | custom-call | tf_op jit(solution)/shard_map/while/body/back_product/pallas_call | solution.py:202
  193.9 5.0 %collective-permute-done.17 = bf16[4,4,16,768]{3,2,1,0:T(8,128)(2,1)S(1)} collective-permute-done((bf16[4,4,16,768]{3,2,1,0:T(8,128)(2,1)S(1)}, bf16[4,4,16,768]{3,2,1,0:T(8,128)(2,1)S(1)}, u32[]{:S(2)}, u32[]{:S(2)}) %collective-permute-start.17) | collective-permute-done | bytes 393248 | tf_op jit(solution)/shard_map/while/body/ppermute | solution.py:19
  201.8 2.4 collective-permute-start.20
  204.9 3.6 %all-to-all-start = ((bf16[8,32,384]{2,1,0:T(8,128)(2,1)}), bf16[8,32,384]{2,1,0:T(8,128)(2,1)S(1)}, u32[]{:S(2)}, u32[]{:S(2)}) async-start(bf16[8,32,384]{2,1,0:T(8,128)(2,1)} %fusion.16), calls=%async_computation | async-start | bytes 393216 | tf_op jit(solution)/shard_map/while/body/all_to_all | solution.py:769
  208.6 4.5 %collective-permute-done.26.refs_2_ = bf16[384,768]{1,0:T(8,128)(2,1)S(1)} collective-permute-done((bf16[384,768]{1,0:T(8,128)(2,1)S(1)}, bf16[384,768]{1,0:T(8,128)(2,1)S(1)}, u32[]{:S(2)}, u32[]{:S(2)}) %collective-permute-start.26) | collective-permute-done | bytes 589856 | tf_op jit(solution)/shard_map/while/body/ppermute | solution.py:19
  217.0 2.2 update.3
  231.9 8.4 %collective-permute-done.60.refs_2_ = bf16[48,3072]{1,0:T(8,128)(2,1)S(1)} collective-permute-done((bf16[48,3072]{1,0:T(8,128)(2,1)S(1)}, bf16[48,3072]{1,0:T(8,128)(2,1)S(1)}, u32[]{:S(2)}, u32[]{:S(2)}) %collective-permute-start.60) | collective-permute-done | bytes 294944 | tf_op jit(solution)/shard_map/ppermute | solution.py:19
  240.3 4.6 %collective-permute-done.61.refs_3_ = bf16[48,3072]{1,0:T(8,128)(2,1)S(1)} collective-permute-done((bf16[48,3072]{1,0:T(8,128)(2,1)S(1)}, bf16[48,3072]{1,0:T(8,128)(2,1)S(1)}, u32[]{:S(2)}, u32[]{:S(2)}) %collective-permute-start.61) | collective-permute-done | bytes 294944 | tf_op jit(solution)/shard_map/ppermute | solution.py:19
  (257 shorter events, 109.2 us)
Async XLA Ops:
  15.1 30.5 %collective-permute-start.39 = (bf16[2,384,768]{2,1,0:T(8,128)(2,1)}, bf16[2,384,768]{2,1,0:T(8,128)(2,1)}, u32[]{:S(2)}, u32[]{:S(2)}) collective-permute-start(bf16[2,384,768]{2,1,0:T(8,128)(2,1)} %get-tuple-element.144), channel_id=1, source_target_pairs={{0,8},{8,0},{16,24},{24,16},{1,9},{9,1},{17,25},{25,17},{2,10},{10... | collective-permute-start | bytes 3538952 | tf_op jit(solution)/shard_map/ppermute | solution.py:19
  15.4 30.2 %collective-permute-start.40 = (bf16[2,384,768]{2,1,0:T(8,128)(2,1)}, bf16[2,384,768]{2,1,0:T(8,128)(2,1)}, u32[]{:S(2)}, u32[]{:S(2)}) collective-permute-start(bf16[2,384,768]{2,1,0:T(8,128)(2,1)} %get-tuple-element.146), channel_id=1, source_target_pairs={{0,8},{8,0},{16,24},{24,16},{1,9},{9,1},{17,25},{25,17},{2,10},{10... | collective-permute-start | bytes 3538952 | tf_op jit(solution)/shard_map/ppermute | solution.py:19
  16.5 12.3 %collective-permute-start.29 = (bf16[64,3072]{1,0:T(8,128)(2,1)S(1)}, bf16[64,3072]{1,0:T(8,128)(2,1)S(1)}, u32[]{:S(2)}, u32[]{:S(2)}) collective-permute-start(bf16[64,3072]{1,0:T(8,128)(2,1)S(1)} %send_blocks.6), channel_id=1, source_target_pairs={{0,16},{8,24},{16,0},{24,8},{1,17},{9,25},{17,1},{25,9},{2,18},{10... | collective-permute-start | bytes 1179656 | tf_op jit(solution)/shard_map/ppermute | solution.py:19
  20.6 17.0 %collective-permute-start.30 = (bf16[2,4,32,768]{3,2,1,0:T(8,128)(2,1)S(1)}, bf16[2,4,32,768]{3,2,1,0:T(8,128)(2,1)S(1)}, u32[]{:S(2)}, u32[]{:S(2)}) collective-permute-start(bf16[2,4,32,768]{3,2,1,0:T(8,128)(2,1)S(1)} %get-tuple-element.141), channel_id=1, source_target_pairs={{0,8},{8,0},{16,24},{24,16},{1,9},{9,1},{17,25},{25,17},{2,10},{10... | collective-permute-start | bytes 1179656 | tf_op jit(solution)/shard_map/ppermute | solution.py:19
  31.5 17.9 %all-to-all-start.2 = ((bf16[8,48,384]{2,1,0:T(8,128)(2,1)}), bf16[8,48,384]{2,1,0:T(8,128)(2,1)S(1)}, u32[]{:S(2)}, u32[]{:S(2)}) async-start(bf16[8,48,384]{2,1,0:T(8,128)(2,1)} %features.2), calls=%async_computation.2 | async-start | bytes 589824 | tf_op jit(solution)/shard_map/all_to_all | solution.py:747
  47.3 34.1 %collective-permute-start.41 = (bf16[384,768]{1,0:T(8,128)(2,1)S(1)}, bf16[384,768]{1,0:T(8,128)(2,1)S(1)}, u32[]{:S(2)}, u32[]{:S(2)}) collective-permute-start(bf16[384,768]{1,0:T(8,128)(2,1)S(1)} %get-tuple-element.147), channel_id=1, source_target_pairs={{0,16},{8,24},{16,0},{24,8},{1,17},{9,25},{17,1},{25,9},{2,18},{10... | collective-permute-start | bytes 1769480 | tf_op jit(solution)/shard_map/ppermute | solution.py:19
  49.1 38.0 %collective-permute-start.47 = (bf16[384,768]{1,0:T(8,128)(2,1)}, bf16[384,768]{1,0:T(8,128)(2,1)S(1)}, u32[]{:S(2)}, u32[]{:S(2)}) collective-permute-start(bf16[384,768]{1,0:T(8,128)(2,1)} %get-tuple-element.152), channel_id=1, source_target_pairs={{0,16},{8,24},{16,0},{24,8},{1,17},{9,25},{17,1},{25,9},{2,18},{10... | collective-permute-start | bytes 1769480 | tf_op jit(solution)/shard_map/ppermute | solution.py:19
  52.6 13.4 %collective-permute-start.35 = (bf16[4,32,768]{2,1,0:T(8,128)(2,1)S(1)}, bf16[4,32,768]{2,1,0:T(8,128)(2,1)S(1)}, u32[]{:S(2)}, u32[]{:S(2)}) collective-permute-start(bf16[4,32,768]{2,1,0:T(8,128)(2,1)S(1)} %choose.1), channel_id=1, source_target_pairs={{0,4},{1,5},{2,6},{3,7},{4,0},{5,1},{6,2},{7,3},{8,12},{9,13},{10,... | collective-permute-start | bytes 589832 | tf_op jit(solution)/shard_map/ppermute | solution.py:19
  68.0 13.4 %collective-permute-start.45 = (bf16[8,48,384]{2,1,0:T(8,128)(2,1)S(1)}, bf16[8,48,384]{2,1,0:T(8,128)(2,1)S(1)}, u32[]{:S(2)}, u32[]{:S(2)}) collective-permute-start(bf16[8,48,384]{2,1,0:T(8,128)(2,1)S(1)} %all-to-all-done.2), channel_id=1, source_target_pairs={{0,16},{8,24},{16,0},{24,8},{1,17},{9,25},{17,1},{25,9},{2,18},{10... | collective-permute-start | bytes 884744 | tf_op jit(solution)/shard_map/ppermute | solution.py:19
  72.1 12.7 %collective-permute-start.44 = (bf16[8,48,384]{2,1,0:T(8,128)(2,1)S(1)}, bf16[8,48,384]{2,1,0:T(8,128)(2,1)S(1)}, u32[]{:S(2)}, u32[]{:S(2)}) collective-permute-start(bf16[8,48,384]{2,1,0:T(8,128)(2,1)S(1)} %all-to-all-done.2), channel_id=1, source_target_pairs={{0,8},{8,0},{16,24},{24,16},{1,9},{9,1},{17,25},{25,17},{2,10},{10... | collective-permute-start | bytes 884744 | tf_op jit(solution)/shard_map/ppermute | solution.py:19
  88.3 12.1 %collective-permute-start.48 = (bf16[4,4,16,768]{3,2,1,0:T(8,128)(2,1)S(1)}, bf16[4,4,16,768]{3,2,1,0:T(8,128)(2,1)S(1)}, u32[]{:S(2)}, u32[]{:S(2)}) collective-permute-start(bf16[4,4,16,768]{3,2,1,0:T(8,128)(2,1)S(1)} %get-tuple-element.154), channel_id=1, source_target_pairs={{0,1},{1,0},{2,3},{3,2},{4,5},{5,4},{6,7},{7,6},{8,9},{9,8},{10,11... | collective-permute-start | bytes 1179656 | tf_op jit(solution)/shard_map/ppermute | solution.py:19
  89.8 22.6 %collective-permute-start.57 = (bf16[384,768]{1,0:T(8,128)(2,1)S(1)}, bf16[384,768]{1,0:T(8,128)(2,1)S(1)}, u32[]{:S(2)}, u32[]{:S(2)}) collective-permute-start(bf16[384,768]{1,0:T(8,128)(2,1)S(1)} %grad_product.2.refs_0_), channel_id=1, source_target_pairs={{0,16},{8,24},{16,0},{24,8},{1,17},{9,25},{17,1},{25,9},{2,18},{10... | collective-permute-start | bytes 1769480 | tf_op jit(solution)/shard_map/ppermute | solution.py:19
  92.6 17.3 %collective-permute-start.43 = (bf16[8,32,384]{2,1,0:T(8,128)(2,1)S(1)}, bf16[8,32,384]{2,1,0:T(8,128)(2,1)S(1)}, u32[]{:S(2)}, u32[]{:S(2)}) collective-permute-start(bf16[8,32,384]{2,1,0:T(8,128)(2,1)S(1)} %slice_bitcast_fusion.12), channel_id=1, source_target_pairs={{0,16},{8,24},{16,0},{24,8},{1,17},{9,25},{17,1},{25,9},{2,18},{10... | collective-permute-start | bytes 589832 | tf_op jit(solution)/shard_map/ppermute | solution.py:19
  100.5 11.9 %collective-permute-start.51 = (bf16[4,16,768]{2,1,0:T(8,128)(2,1)S(1)}, bf16[4,16,768]{2,1,0:T(8,128)(2,1)S(1)}, u32[]{:S(2)}, u32[]{:S(2)}) collective-permute-start(bf16[4,16,768]{2,1,0:T(8,128)(2,1)S(1)} %get-tuple-element.214), channel_id=1, source_target_pairs={{0,6},{1,7},{2,4},{3,5},{4,2},{5,3},{6,0},{7,1},{8,14},{9,15},{10,... | collective-permute-start | bytes 294920 | tf_op jit(solution)/shard_map/ppermute | solution.py:19
  112.4 15.9 %collective-permute-start.56 = (bf16[384,768]{1,0:T(8,128)(2,1)S(1)}, bf16[384,768]{1,0:T(8,128)(2,1)S(1)}, u32[]{:S(2)}, u32[]{:S(2)}) collective-permute-start(bf16[384,768]{1,0:T(8,128)(2,1)S(1)} %grad_product.2.refs_0_), channel_id=1, source_target_pairs={{0,8},{8,0},{16,24},{24,16},{1,9},{9,1},{17,25},{25,17},{2,10},{10... | collective-permute-start | bytes 1769480 | tf_op jit(solution)/shard_map/ppermute | solution.py:19
  112.4 16.8 %collective-permute-start.58 = (bf16[384,768]{1,0:T(8,128)(2,1)S(1)}, bf16[384,768]{1,0:T(8,128)(2,1)S(1)}, u32[]{:S(2)}, u32[]{:S(2)}) collective-permute-start(bf16[384,768]{1,0:T(8,128)(2,1)S(1)} %collective-permute-done.57.refs_2_), channel_id=1, source_target_pairs={{0,8},{8,0},{16,24},{24,16},{1,9},{9,1},{17,25},{25,17},{2,10},{10... | collective-permute-start | bytes 1769480 | tf_op jit(solution)/shard_map/ppermute | solution.py:19
  113.0 13.8 %all-to-all-start.3 = ((bf16[8,32,384]{2,1,0:T(8,128)(2,1)}), bf16[8,32,384]{2,1,0:T(8,128)(2,1)S(1)}, u32[]{:S(2)}, u32[]{:S(2)}) async-start(bf16[8,32,384]{2,1,0:T(8,128)(2,1)} %fusion.4), calls=%async_computation.3 | async-start | bytes 393216 | tf_op jit(solution)/shard_map/all_to_all | solution.py:769
  141.0 11.7 %collective-permute-start.4 = (bf16[4,32,768]{2,1,0:T(8,128)(2,1)}, bf16[4,32,768]{2,1,0:T(8,128)(2,1)S(1)}, u32[]{:S(2)}, u32[]{:S(2)}) collective-permute-start(bf16[4,32,768]{2,1,0:T(8,128)(2,1)} %pad_maximum_fusion.8), channel_id=1, source_target_pairs={{0,6},{1,7},{2,4},{3,5},{4,2},{5,3},{6,0},{7,1},{8,14},{9,15},{10,... | collective-permute-start | bytes 589832 | tf_op jit(solution)/shard_map/while/body/ppermute | solution.py:19
  143.3 19.7 %collective-permute-start.5 = (bf16[4,32,768]{2,1,0:T(8,128)(2,1)}, bf16[4,32,768]{2,1,0:T(8,128)(2,1)}, u32[]{:S(2)}, u32[]{:S(2)}) collective-permute-start(bf16[4,32,768]{2,1,0:T(8,128)(2,1)} %pad_maximum_fusion.8), channel_id=1, source_target_pairs={{0,1},{1,0},{2,3},{3,2},{4,5},{5,4},{6,7},{7,6},{8,9},{9,8},{10,11... | collective-permute-start | bytes 589832 | tf_op jit(solution)/shard_map/while/body/ppermute | solution.py:19
  146.6 33.1 %collective-permute-start.10 = (bf16[384,768]{1,0:T(8,128)(2,1)}, bf16[384,768]{1,0:T(8,128)(2,1)S(1)}, u32[]{:S(2)}, u32[]{:S(2)}) collective-permute-start(bf16[384,768]{1,0:T(8,128)(2,1)} %get-tuple-element.352), channel_id=1, source_target_pairs={{0,16},{8,24},{16,0},{24,8},{1,17},{9,25},{17,1},{25,9},{2,18},{10... | collective-permute-start | bytes 1769480 | tf_op jit(solution)/shard_map/while/body/ppermute | solution.py:19
  147.8 38.9 %collective-permute-start.16 = (bf16[384,768]{1,0:T(8,128)(2,1)}, bf16[384,768]{1,0:T(8,128)(2,1)S(1)}, u32[]{:S(2)}, u32[]{:S(2)}) collective-permute-start(bf16[384,768]{1,0:T(8,128)(2,1)} %get-tuple-element.357), channel_id=1, source_target_pairs={{0,16},{8,24},{16,0},{24,8},{1,17},{9,25},{17,1},{25,9},{2,18},{10... | collective-permute-start | bytes 1769480 | tf_op jit(solution)/shard_map/while/body/ppermute | solution.py:19
  148.8 18.3 %collective-permute-start.7 = (bf16[4,32,768]{2,1,0:T(8,128)(2,1)}, bf16[4,32,768]{2,1,0:T(8,128)(2,1)}, u32[]{:S(2)}, u32[]{:S(2)}) collective-permute-start(bf16[4,32,768]{2,1,0:T(8,128)(2,1)} %pad_maximum_fusion.8), channel_id=1, source_target_pairs={{0,4},{1,5},{2,6},{3,7},{4,0},{5,1},{6,2},{7,3},{8,12},{9,13},{10,... | collective-permute-start | bytes 589832 | tf_op jit(solution)/shard_map/while/body/ppermute | solution.py:19
  153.4 13.7 %collective-permute-start.6 = (bf16[4,32,768]{2,1,0:T(8,128)(2,1)}, bf16[4,32,768]{2,1,0:T(8,128)(2,1)}, u32[]{:S(2)}, u32[]{:S(2)}) collective-permute-start(bf16[4,32,768]{2,1,0:T(8,128)(2,1)} %collective-permute-done.3), channel_id=1, source_target_pairs={{0,1},{1,0},{2,3},{3,2},{4,5},{5,4},{6,7},{7,6},{8,9},{9,8},{10,11... | collective-permute-start | bytes 589832 | tf_op jit(solution)/shard_map/while/body/ppermute | solution.py:19
  154.5 17.3 %all-to-all-start.1 = ((bf16[8,48,384]{2,1,0:T(8,128)(2,1)}), bf16[8,48,384]{2,1,0:T(8,128)(2,1)}, u32[]{:S(2)}, u32[]{:S(2)}) async-start(bf16[8,48,384]{2,1,0:T(8,128)(2,1)} %features.3), calls=%async_computation.1 | async-start | bytes 589824 | tf_op jit(solution)/shard_map/while/body/all_to_all | solution.py:747
  165.0 14.8 %collective-permute-start.9 = (bf16[4,32,768]{2,1,0:T(8,128)(2,1)}, bf16[4,32,768]{2,1,0:T(8,128)(2,1)S(1)}, u32[]{:S(2)}, u32[]{:S(2)}) collective-permute-start(bf16[4,32,768]{2,1,0:T(8,128)(2,1)} %copy-done.30), channel_id=1, source_target_pairs={{0,1},{1,0},{2,3},{3,2},{4,5},{5,4},{6,7},{7,6},{8,9},{9,8},{10,11... | collective-permute-start | bytes 589832 | tf_op jit(solution)/shard_map/while/body/ppermute | solution.py:19
  184.9 32.1 %collective-permute-start.24 = (bf16[64,3072]{1,0:T(8,128)(2,1)}, bf16[64,3072]{1,0:T(8,128)(2,1)S(1)}, u32[]{:S(2)}, u32[]{:S(2)}) collective-permute-start(bf16[64,3072]{1,0:T(8,128)(2,1)} %send_blocks.11), channel_id=1, source_target_pairs={{0,16},{8,24},{16,0},{24,8},{1,17},{9,25},{17,1},{25,9},{2,18},{10... | collective-permute-start | bytes 1179656 | tf_op jit(solution)/shard_map/while/body/ppermute | solution.py:19
  189.7 12.1 %collective-permute-start.12 = (bf16[8,32,384]{2,1,0:T(8,128)(2,1)S(1)}, bf16[8,32,384]{2,1,0:T(8,128)(2,1)S(1)}, u32[]{:S(2)}, u32[]{:S(2)}) collective-permute-start(bf16[8,32,384]{2,1,0:T(8,128)(2,1)S(1)} %slice_bitcast_fusion.23), channel_id=1, source_target_pairs={{0,16},{8,24},{16,0},{24,8},{1,17},{9,25},{17,1},{25,9},{2,18},{10... | collective-permute-start | bytes 589832 | tf_op jit(solution)/shard_map/while/body/ppermute | solution.py:19
  193.0 20.1 %collective-permute-start.26 = (bf16[384,768]{1,0:T(8,128)(2,1)S(1)}, bf16[384,768]{1,0:T(8,128)(2,1)S(1)}, u32[]{:S(2)}, u32[]{:S(2)}) collective-permute-start(bf16[384,768]{1,0:T(8,128)(2,1)S(1)} %grad_product.3.refs_0_), channel_id=1, source_target_pairs={{0,16},{8,24},{16,0},{24,8},{1,17},{9,25},{17,1},{25,9},{2,18},{10... | collective-permute-start | bytes 1769480 | tf_op jit(solution)/shard_map/while/body/ppermute | solution.py:19
  201.2 11.9 %collective-permute-start.19 = (bf16[4,16,768]{2,1,0:T(8,128)(2,1)}, bf16[4,16,768]{2,1,0:T(8,128)(2,1)}, u32[]{:S(2)}, u32[]{:S(2)}) collective-permute-start(bf16[4,16,768]{2,1,0:T(8,128)(2,1)} %get-tuple-element.361), channel_id=1, source_target_pairs={{0,4},{1,5},{2,6},{3,7},{4,0},{5,1},{6,2},{7,3},{8,12},{9,13},{10,... | collective-permute-start | bytes 294920 | tf_op jit(solution)/shard_map/while/body/ppermute | solution.py:19
  204.9 12.1 %all-to-all-start = ((bf16[8,32,384]{2,1,0:T(8,128)(2,1)}), bf16[8,32,384]{2,1,0:T(8,128)(2,1)S(1)}, u32[]{:S(2)}, u32[]{:S(2)}) async-start(bf16[8,32,384]{2,1,0:T(8,128)(2,1)} %fusion.16), calls=%async_computation | async-start | bytes 393216 | tf_op jit(solution)/shard_map/while/body/all_to_all | solution.py:769
  208.5 16.0 %collective-permute-start.25 = (bf16[384,768]{1,0:T(8,128)(2,1)S(1)}, bf16[384,768]{1,0:T(8,128)(2,1)S(1)}, u32[]{:S(2)}, u32[]{:S(2)}) collective-permute-start(bf16[384,768]{1,0:T(8,128)(2,1)S(1)} %grad_product.3.refs_0_), channel_id=1, source_target_pairs={{0,8},{8,0},{16,24},{24,16},{1,9},{9,1},{17,25},{25,17},{2,10},{10... | collective-permute-start | bytes 1769480 | tf_op jit(solution)/shard_map/while/body/ppermute | solution.py:19
  230.8 14.0 %collective-permute-start.61 = (bf16[48,3072]{1,0:T(8,128)(2,1)S(1)}, bf16[48,3072]{1,0:T(8,128)(2,1)S(1)}, u32[]{:S(2)}, u32[]{:S(2)}) collective-permute-start(bf16[48,3072]{1,0:T(8,128)(2,1)S(1)} %get-tuple-element.165), channel_id=1, source_target_pairs={{0,24},{8,16},{16,8},{24,0},{1,25},{9,17},{17,9},{25,1},{2,26},{10... | collective-permute-start | bytes 884744 | tf_op jit(solution)/shard_map/ppermute | solution.py:19
  (75 other events, 521.2 us)
where the time goes:
time: 248 us; the launch traced here: 247 us
  waiting for transfers between devices  84.5 us (34%)
  starting transfers between devices  82.3 us (33%)
  Pallas kernels  49.8 us (20%)
  local copies, waits for them, and re-layouts  20.9 us (8%)
  other arithmetic  5.85 us (2%)
    ppermute x62, waiting for transfers between devices, swap(): return lax.ppermute(block, axis, [(i, i ^ bits) for i in range(size)])  81.8 us
    ppermute x62, starting transfers between devices, swap(): return lax.ppermute(block, axis, [(i, i ^ bits) for i in range(size)])  59.4 us
    pallas_call x31, Pallas kernels, call(): pl.pallas_call(body, in_specs=spaces, out_specs=out_spaces, out_shape=out...  49.8 us
    all_to_all x2, starting transfers between devices, to_groups(): return lax.all_to_all(blocks, 'fsdp', 0, 0, tiled=True)  14.7 us
    unnamed x51, local copies, waits for them, and re-layouts  9.51 us
    all_to_all x2, starting transfers between devices, stage(): dn = lax.all_to_all(sum_halves(*dn, 'section'), 'fsdp', 0, 0, tiled=True)  8.19 us
    while x46, local copies, waits for them, and re-layouts  7.51 us
  transfers between devices with their start and end apart: 66, of which 20 were waited for; matrix products, arithmetic and copies ran while one was open for 6% of the time, Pallas kernels for 17%

commit v1 on v0

--- a/solution.py
+++ b/solution.py
@@ -757,7 +757,7 @@
         else:
             came = across(where, plan, place, (where.ahead, where.back), (low, weight))
             line = [slopes] + [swap(slopes, "fsdp", bits) for bits in (2, 4, 6)]
-            line[1], line[3], inputs, hidden = fence(line[1], line[3], inputs, hidden)
+            line[3], inputs, hidden = fence(line[3], inputs, hidden)
             feats = to_groups(features(inputs, hidden, groups))
             slopes = jnp.stack([b for near in line for b in (near, swap(near, "fsdp", 1))])
         low_came, weight_came = came

time: 248 us -> 249 us (level)
  waiting for transfers between devices: 84.5 us -> 88.4 us
    ppermute x62, waiting for transfers between devices: 81.8 us -> 88.2 us  [swap(): return lax.ppermute(block, axis, [(i, i ^ bits) for i in range(size)])]
    all_to_all x2, starting transfers between devices: 14.7 us -> 10.3 us  [to_groups(): return lax.all_to_all(blocks, 'fsdp', 0, 0, tiled=True)]
    all_to_all x2, waiting for transfers between devices: 2.7 us -> 0.01 us  [to_groups(): return lax.all_to_all(blocks, 'fsdp', 0, 0, tiled=True)]
  transfers between devices with their start and end apart: 66 -> 66, of which waited for: 20 -> 21; matrix products, arithmetic and copies ran while one was open for 6% -> 5% of each run, Pallas kernels for 17% -> 17%
where the time goes in v1:
time: 249 us; the launch traced here: 248 us
  waiting for transfers between devices  88.4 us (36%)
  starting transfers between devices  80.4 us (32%)
  Pallas kernels  50.5 us (20%)
  local copies, waits for them, and re-layouts  19.3 us (8%)
  other arithmetic  5.85 us (2%)
    ppermute x62, waiting for transfers between devices, swap(): return lax.ppermute(block, axis, [(i, i ^ bits) for i in range(size)])  88.2 us
    ppermute x62, starting transfers between devices, swap(): return lax.ppermute(block, axis, [(i, i ^ bits) for i in range(size)])  61.5 us
    pallas_call x31, Pallas kernels, call(): pl.pallas_call(body, in_specs=spaces, out_specs=out_spaces, out_shape=out...  50.5 us
    all_to_all x2, starting transfers between devices, to_groups(): return lax.all_to_all(blocks, 'fsdp', 0, 0, tiled=True)  10.3 us
    unnamed x51, local copies, waits for them, and re-layouts  9.51 us
    all_to_all x2, starting transfers between devices, stage(): dn = lax.all_to_all(sum_halves(*dn, 'section'), 'fsdp', 0, 0, tiled=True)  8.61 us
    while x46, local copies, waits for them, and re-layouts  5.89 us
  transfers between devices with their start and end apart: 66, of which 21 were waited for; matrix products, arithmetic and copies ran while one was open for 5% of the time, Pallas kernels for 17%

profile of v1, /device:TPU:0, one launch (start us, length us, event | category | flops | bytes accessed | tf_op | source)
XLA Modules:
  0.0 247.7 jit_solution(16748807488096999708)
XLA Ops:
  10.0 5.1 %split_weights.1 = (f32[384,3072]{1,0:T(8,128)}, bf16[2,384,768]{2,1,0:T(8,128)(2,1)}, bf16[2,384,768]{2,1,0:T(8,128)(2,1)}, bf16[2,384,768]{2,1,0:T(8,128)(2,1)}, bf16[2,384,768]{2,1,0:T(8,128)(2,1)}) custom-call(s32[21]{0:T(128)S(1)} %make_plan.1.plan, bf16[384,3072]{1,0:T(8,128)(2,1)S(1)} %bitcast.166, f32[384,3072]{1,0:T(8,128)S(1)} %bitcast.163), custom_call_target="tpu_custom_call" | custom-call | tf_op jit(solution)/shard_map/split_weights/pallas_call | solution.py:202
  16.5 2.7 %collective-permute-start.29 = (bf16[64,3072]{1,0:T(8,128)(2,1)S(1)}, bf16[64,3072]{1,0:T(8,128)(2,1)S(1)}, u32[]{:S(2)}, u32[]{:S(2)}) collective-permute-start(bf16[64,3072]{1,0:T(8,128)(2,1)S(1)} %send_blocks.6), channel_id=1, source_target_pairs={{0,16},{8,24},{16,0},{24,8},{1,17},{9,25},{17,1},{25,9},{2,18},{10... | collective-permute-start | bytes 1179656 | tf_op jit(solution)/shard_map/ppermute | solution.py:19
  20.7 8.1 %collective-permute-done.29.came = bf16[64,3072]{1,0:T(8,128)(2,1)S(1)} collective-permute-done((bf16[64,3072]{1,0:T(8,128)(2,1)S(1)}, bf16[64,3072]{1,0:T(8,128)(2,1)S(1)}, u32[]{:S(2)}, u32[]{:S(2)}) %collective-permute-start.29) | collective-permute-done | bytes 393248 | tf_op jit(solution)/shard_map/ppermute | solution.py:19
  31.5 6.1 %all-to-all-start.2 = ((bf16[8,48,384]{2,1,0:T(8,128)(2,1)}), bf16[8,48,384]{2,1,0:T(8,128)(2,1)S(1)}, u32[]{:S(2)}, u32[]{:S(2)}) async-start(bf16[8,48,384]{2,1,0:T(8,128)(2,1)} %features.2), calls=%async_computation.2 | async-start | bytes 589824 | tf_op jit(solution)/shard_map/all_to_all | solution.py:747
  40.0 4.8 %collective-permute-done.31.came = bf16[4,32,768]{2,1,0:T(8,128)(2,1)S(1)} collective-permute-done((bf16[4,32,768]{2,1,0:T(8,128)(2,1)S(1)}, bf16[4,32,768]{2,1,0:T(8,128)(2,1)S(1)}, u32[]{:S(2)}, u32[]{:S(2)}) %collective-permute-start.31) | collective-permute-done | bytes 196640 | tf_op jit(solution)/shard_map/ppermute | solution.py:19
  52.6 2.4 collective-permute-start.35
  55.0 5.2 %collective-permute-done.33 = bf16[4,32,768]{2,1,0:T(8,128)(2,1)S(1)} collective-permute-done((bf16[4,32,768]{2,1,0:T(8,128)(2,1)S(1)}, bf16[4,32,768]{2,1,0:T(8,128)(2,1)S(1)}, u32[]{:S(2)}, u32[]{:S(2)}) %collective-permute-start.33) | collective-permute-done | bytes 196640 | tf_op jit(solution)/shard_map/ppermute | solution.py:19
  60.8 2.8 %collective-permute-start.37 = (bf16[4,32,768]{2,1,0:T(8,128)(2,1)S(1)}, bf16[4,32,768]{2,1,0:T(8,128)(2,1)S(1)}, u32[]{:S(2)}, u32[]{:S(2)}) collective-permute-start(bf16[4,32,768]{2,1,0:T(8,128)(2,1)S(1)} %choose.1), channel_id=1, source_target_pairs={{0,6},{1,7},{2,4},{3,5},{4,2},{5,3},{6,0},{7,1},{8,14},{9,15},{10,... | collective-permute-start | bytes 589832 | tf_op jit(solution)/shard_map/ppermute | solution.py:19
  63.6 2.4 collective-permute-done.35
  72.2 9.2 %collective-permute-done.45 = bf16[8,48,384]{2,1,0:T(8,128)(2,1)S(1)} collective-permute-done((bf16[8,48,384]{2,1,0:T(8,128)(2,1)S(1)}, bf16[8,48,384]{2,1,0:T(8,128)(2,1)S(1)}, u32[]{:S(2)}, u32[]{:S(2)}) %collective-permute-start.45) | collective-permute-done | bytes 294944 | tf_op jit(solution)/shard_map/ppermute | solution.py:19
  89.8 2.7 %collective-permute-start.57 = (bf16[384,768]{1,0:T(8,128)(2,1)S(1)}, bf16[384,768]{1,0:T(8,128)(2,1)S(1)}, u32[]{:S(2)}, u32[]{:S(2)}) collective-permute-start(bf16[384,768]{1,0:T(8,128)(2,1)S(1)} %grad_product.2.refs_0_), channel_id=1, source_target_pairs={{0,16},{8,24},{16,0},{24,8},{1,17},{9,25},{17,1},{25,9},{2,18},{10... | collective-permute-start | bytes 1769480 | tf_op jit(solution)/shard_map/ppermute | solution.py:19
  92.7 7.7 %collective-permute-done.48 = bf16[4,4,16,768]{3,2,1,0:T(8,128)(2,1)S(1)} collective-permute-done((bf16[4,4,16,768]{3,2,1,0:T(8,128)(2,1)S(1)}, bf16[4,4,16,768]{3,2,1,0:T(8,128)(2,1)S(1)}, u32[]{:S(2)}, u32[]{:S(2)}) %collective-permute-start.48) | collective-permute-done | bytes 393248 | tf_op jit(solution)/shard_map/ppermute | solution.py:19
  100.5 3.3 %collective-permute-start.51 = (bf16[4,16,768]{2,1,0:T(8,128)(2,1)S(1)}, bf16[4,16,768]{2,1,0:T(8,128)(2,1)S(1)}, u32[]{:S(2)}, u32[]{:S(2)}) collective-permute-start(bf16[4,16,768]{2,1,0:T(8,128)(2,1)S(1)} %get-tuple-element.213), channel_id=1, source_target_pairs={{0,6},{1,7},{2,4},{3,5},{4,2},{5,3},{6,0},{7,1},{8,14},{9,15},{10,... | collective-permute-start | bytes 294920 | tf_op jit(solution)/shard_map/ppermute | solution.py:19
  105.0 5.0 %collective-permute-done.43 = bf16[8,32,384]{2,1,0:T(8,128)(2,1)S(1)} collective-permute-done((bf16[8,32,384]{2,1,0:T(8,128)(2,1)S(1)}, bf16[8,32,384]{2,1,0:T(8,128)(2,1)S(1)}, u32[]{:S(2)}, u32[]{:S(2)}) %collective-permute-start.43) | collective-permute-done | bytes 196640 | tf_op jit(solution)/shard_map/ppermute | solution.py:19
  113.0 4.6 %all-to-all-start.3 = ((bf16[8,32,384]{2,1,0:T(8,128)(2,1)}), bf16[8,32,384]{2,1,0:T(8,128)(2,1)S(1)}, u32[]{:S(2)}, u32[]{:S(2)}) async-start(bf16[8,32,384]{2,1,0:T(8,128)(2,1)} %fusion.4), calls=%async_computation.3 | async-start | bytes 393216 | tf_op jit(solution)/shard_map/all_to_all | solution.py:769
  121.7 2.3 take_rows.4
  131.5 97.1 %while.22 = (s32[]{:T(128)}, bf16[32,3072]{1,0:T(8,128)(2,1)S(1)}, bf16[16,3072]{1,0:T(8,128)(2,1)}, bf16[32,3072]{1,0:T(8,128)(2,1)}, bf16[32,3072]{1,0:T(8,128...) while((s32[]{:T(128)}, bf16[32,3072]{1,0:T(8,128)(2,1)S(1)}, ...), condition=%wide.region_1.0_spmd, body=%wide.region_0.0_spmd.sunk | while | flops 5357570 | bytes 86411120 | solution.py:815
  139.8 3.0 %collective-permute-start.3 = (bf16[4,32,768]{2,1,0:T(8,128)(2,1)}, bf16[4,32,768]{2,1,0:T(8,128)(2,1)S(1)}, u32[]{:S(2)}, u32[]{:S(2)}) collective-permute-start(bf16[4,32,768]{2,1,0:T(8,128)(2,1)} %pad_maximum_fusion.8), channel_id=1, source_target_pairs={{0,6},{1,7},{2,4},{3,5},{4,2},{5,3},{6,0},{7,1},{8,14},{9,15},{10,... | collective-permute-start | bytes 589832 | tf_op jit(solution)/shard_map/while/body/ppermute | solution.py:19
  143.4 2.7 %send_blocks.10 = (bf16[384,768]{1,0:T(8,128)(2,1)}, bf16[384,768]{1,0:T(8,128)(2,1)}) custom-call(s32[21]{0:T(128)S(1)} %get-tuple-element.414.plan, s32[1]{0:T(128)} %bitcast.151.place, bf16[2,384,768]{2,1,0:T(8,128)(2,1)} %get-tuple-element.415.refs_0_.near, bf16[2,384,768]{2,1,0:T(8,128)(2,1)} %get-tuple-element.416.refs_1_.far, ...), custom_call_target="tpu_custom_call" | custom-call | tf_op jit(solution)/shard_map/while/body/send_blocks/pallas_call | solution.py:202
  149.7 2.6 %collective-permute-start.7 = (bf16[4,32,768]{2,1,0:T(8,128)(2,1)}, bf16[4,32,768]{2,1,0:T(8,128)(2,1)}, u32[]{:S(2)}, u32[]{:S(2)}) collective-permute-start(bf16[4,32,768]{2,1,0:T(8,128)(2,1)} %pad_maximum_fusion.8), channel_id=1, source_target_pairs={{0,4},{1,5},{2,6},{3,7},{4,0},{5,1},{6,2},{7,3},{8,12},{9,13},{10,... | collective-permute-start | bytes 589832 | tf_op jit(solution)/shard_map/while/body/ppermute | solution.py:19
  153.2 4.2 %all-to-all-start.1 = ((bf16[8,48,384]{2,1,0:T(8,128)(2,1)}), bf16[8,48,384]{2,1,0:T(8,128)(2,1)}, u32[]{:S(2)}, u32[]{:S(2)}) async-start(bf16[8,48,384]{2,1,0:T(8,128)(2,1)} %features.3), calls=%async_computation.1 | async-start | bytes 589824 | tf_op jit(solution)/shard_map/while/body/all_to_all | solution.py:747
  163.2 8.0 %collective-permute-done.6 = bf16[4,32,768]{2,1,0:T(8,128)(2,1)S(1)} collective-permute-done((bf16[4,32,768]{2,1,0:T(8,128)(2,1)}, bf16[4,32,768]{2,1,0:T(8,128)(2,1)S(1)}, u32[]{:S(2)}, u32[]{:S(2)}) %collective-permute-start.6) | collective-permute-done | bytes 196640 | tf_op jit(solution)/shard_map/while/body/ppermute | solution.py:19
  172.2 2.9 %collective-permute-start.13 = (bf16[8,48,384]{2,1,0:T(8,128)(2,1)}, bf16[8,48,384]{2,1,0:T(8,128)(2,1)S(1)}, u32[]{:S(2)}, u32[]{:S(2)}) collective-permute-start(bf16[8,48,384]{2,1,0:T(8,128)(2,1)} %all-to-all-done.1), channel_id=1, source_target_pairs={{0,16},{8,24},{16,0},{24,8},{1,17},{9,25},{17,1},{25,9},{2,18},{10... | collective-permute-start | bytes 884744 | tf_op jit(solution)/shard_map/while/body/ppermute | solution.py:19
  176.1 3.9 %collective-permute-done.13 = bf16[8,48,384]{2,1,0:T(8,128)(2,1)S(1)} collective-permute-done((bf16[8,48,384]{2,1,0:T(8,128)(2,1)}, bf16[8,48,384]{2,1,0:T(8,128)(2,1)S(1)}, u32[]{:S(2)}, u32[]{:S(2)}) %collective-permute-start.13) | collective-permute-done | bytes 294944 | tf_op jit(solution)/shard_map/while/body/ppermute | solution.py:19
  180.0 3.0 %back_product.3 = (bf16[2,8,32,384]{3,2,1,0:T(8,128)(2,1)S(1)}, bf16[2,8,32,384]{3,2,1,0:T(8,128)(2,1)S(1)}) custom-call(s32[21]{0:T(128)S(1)} %get-tuple-element.414.plan, s32[1]{0:T(128)} %bitcast.151.place, bf16[8,4,32,768]{3,2,1,0:T(8,128)(2,1)S(1)} %bitcast_dynamic-update-slice_fusion.31.slopes_ref, ...), custom_call_target="tpu_custom_call" | custom-call | tf_op jit(solution)/shard_map/while/body/back_product/pallas_call | solution.py:202
  193.9 5.7 %collective-permute-done.17 = bf16[4,4,16,768]{3,2,1,0:T(8,128)(2,1)S(1)} collective-permute-done((bf16[4,4,16,768]{3,2,1,0:T(8,128)(2,1)S(1)}, bf16[4,4,16,768]{3,2,1,0:T(8,128)(2,1)S(1)}, u32[]{:S(2)}, u32[]{:S(2)}) %collective-permute-start.17) | collective-permute-done | bytes 393248 | tf_op jit(solution)/shard_map/while/body/ppermute | solution.py:19
  200.5 2.5 %collective-permute-start.18 = (bf16[4,16,768]{2,1,0:T(8,128)(2,1)S(1)}, bf16[4,16,768]{2,1,0:T(8,128)(2,1)}, u32[]{:S(2)}, u32[]{:S(2)}) collective-permute-start(bf16[4,16,768]{2,1,0:T(8,128)(2,1)S(1)} %get-tuple-element.357), channel_id=1, source_target_pairs={{0,6},{1,7},{2,4},{3,5},{4,2},{5,3},{6,0},{7,1},{8,14},{9,15},{10,... | collective-permute-start | bytes 294920 | tf_op jit(solution)/shard_map/while/body/ppermute | solution.py:19
  205.6 4.1 %all-to-all-start = ((bf16[8,32,384]{2,1,0:T(8,128)(2,1)}), bf16[8,32,384]{2,1,0:T(8,128)(2,1)S(1)}, u32[]{:S(2)}, u32[]{:S(2)}) async-start(bf16[8,32,384]{2,1,0:T(8,128)(2,1)} %fusion.16), calls=%async_computation | async-start | bytes 393216 | tf_op jit(solution)/shard_map/while/body/all_to_all | solution.py:769
  209.8 3.6 %collective-permute-done.26.refs_2_ = bf16[384,768]{1,0:T(8,128)(2,1)S(1)} collective-permute-done((bf16[384,768]{1,0:T(8,128)(2,1)S(1)}, bf16[384,768]{1,0:T(8,128)(2,1)S(1)}, u32[]{:S(2)}, u32[]{:S(2)}) %collective-permute-start.26) | collective-permute-done | bytes 589856 | tf_op jit(solution)/shard_map/while/body/ppermute | solution.py:19
  219.7 2.5 %take_rows.5 = (bf16[32,3072]{1,0:T(8,128)(2,1)}, bf16[32,3072]{1,0:T(8,128)(2,1)}) custom-call(s32[21]{0:T(128)S(1)} %get-tuple-element.414.plan, s32[1]{0:T(128)S(6)} %add.104.place, bf16[2,64,3072]{2,1,0:T(8,128)(2,1)S(1)} %copy-done.19, bf16[2,64,3072]{2,1,0:T(8,128)(2,1)} %get-tuple-element.420.refs_1_.far, ...), custom_call_target="tpu_custom_call" | custom-call | tf_op jit(solution)/shard_map/while/body/take_rows/pallas_call | solution.py:202
  232.5 8.0 %collective-permute-done.60.refs_2_ = bf16[48,3072]{1,0:T(8,128)(2,1)S(1)} collective-permute-done((bf16[48,3072]{1,0:T(8,128)(2,1)S(1)}, bf16[48,3072]{1,0:T(8,128)(2,1)S(1)}, u32[]{:S(2)}, u32[]{:S(2)}) %collective-permute-start.60) | collective-permute-done | bytes 294944 | tf_op jit(solution)/shard_map/ppermute | solution.py:19
  240.5 5.4 %collective-permute-done.61.refs_3_ = bf16[48,3072]{1,0:T(8,128)(2,1)S(1)} collective-permute-done((bf16[48,3072]{1,0:T(8,128)(2,1)S(1)}, bf16[48,3072]{1,0:T(8,128)(2,1)S(1)}, u32[]{:S(2)}, u32[]{:S(2)}) %collective-permute-start.61) | collective-permute-done | bytes 294944 | tf_op jit(solution)/shard_map/ppermute | solution.py:19
  (257 shorter events, 108.3 us)
Async XLA Ops:
  15.1 30.5 %collective-permute-start.39 = (bf16[2,384,768]{2,1,0:T(8,128)(2,1)}, bf16[2,384,768]{2,1,0:T(8,128)(2,1)}, u32[]{:S(2)}, u32[]{:S(2)}) collective-permute-start(bf16[2,384,768]{2,1,0:T(8,128)(2,1)} %get-tuple-element.143), channel_id=1, source_target_pairs={{0,8},{8,0},{16,24},{24,16},{1,9},{9,1},{17,25},{25,17},{2,10},{10... | collective-permute-start | bytes 3538952 | tf_op jit(solution)/shard_map/ppermute | solution.py:19
  15.4 30.2 %collective-permute-start.40 = (bf16[2,384,768]{2,1,0:T(8,128)(2,1)}, bf16[2,384,768]{2,1,0:T(8,128)(2,1)}, u32[]{:S(2)}, u32[]{:S(2)}) collective-permute-start(bf16[2,384,768]{2,1,0:T(8,128)(2,1)} %get-tuple-element.145), channel_id=1, source_target_pairs={{0,8},{8,0},{16,24},{24,16},{1,9},{9,1},{17,25},{25,17},{2,10},{10... | collective-permute-start | bytes 3538952 | tf_op jit(solution)/shard_map/ppermute | solution.py:19
  16.5 12.3 %collective-permute-start.29 = (bf16[64,3072]{1,0:T(8,128)(2,1)S(1)}, bf16[64,3072]{1,0:T(8,128)(2,1)S(1)}, u32[]{:S(2)}, u32[]{:S(2)}) collective-permute-start(bf16[64,3072]{1,0:T(8,128)(2,1)S(1)} %send_blocks.6), channel_id=1, source_target_pairs={{0,16},{8,24},{16,0},{24,8},{1,17},{9,25},{17,1},{25,9},{2,18},{10... | collective-permute-start | bytes 1179656 | tf_op jit(solution)/shard_map/ppermute | solution.py:19
  20.6 17.0 %collective-permute-start.30 = (bf16[2,4,32,768]{3,2,1,0:T(8,128)(2,1)S(1)}, bf16[2,4,32,768]{3,2,1,0:T(8,128)(2,1)S(1)}, u32[]{:S(2)}, u32[]{:S(2)}) collective-permute-start(bf16[2,4,32,768]{3,2,1,0:T(8,128)(2,1)S(1)} %get-tuple-element.140), channel_id=1, source_target_pairs={{0,8},{8,0},{16,24},{24,16},{1,9},{9,1},{17,25},{25,17},{2,10},{10... | collective-permute-start | bytes 1179656 | tf_op jit(solution)/shard_map/ppermute | solution.py:19
  31.5 17.9 %all-to-all-start.2 = ((bf16[8,48,384]{2,1,0:T(8,128)(2,1)}), bf16[8,48,384]{2,1,0:T(8,128)(2,1)S(1)}, u32[]{:S(2)}, u32[]{:S(2)}) async-start(bf16[8,48,384]{2,1,0:T(8,128)(2,1)} %features.2), calls=%async_computation.2 | async-start | bytes 589824 | tf_op jit(solution)/shard_map/all_to_all | solution.py:747
  47.3 34.1 %collective-permute-start.41 = (bf16[384,768]{1,0:T(8,128)(2,1)S(1)}, bf16[384,768]{1,0:T(8,128)(2,1)S(1)}, u32[]{:S(2)}, u32[]{:S(2)}) collective-permute-start(bf16[384,768]{1,0:T(8,128)(2,1)S(1)} %get-tuple-element.146), channel_id=1, source_target_pairs={{0,16},{8,24},{16,0},{24,8},{1,17},{9,25},{17,1},{25,9},{2,18},{10... | collective-permute-start | bytes 1769480 | tf_op jit(solution)/shard_map/ppermute | solution.py:19
  49.1 38.0 %collective-permute-start.47 = (bf16[384,768]{1,0:T(8,128)(2,1)}, bf16[384,768]{1,0:T(8,128)(2,1)S(1)}, u32[]{:S(2)}, u32[]{:S(2)}) collective-permute-start(bf16[384,768]{1,0:T(8,128)(2,1)} %get-tuple-element.151), channel_id=1, source_target_pairs={{0,16},{8,24},{16,0},{24,8},{1,17},{9,25},{17,1},{25,9},{2,18},{10... | collective-permute-start | bytes 1769480 | tf_op jit(solution)/shard_map/ppermute | solution.py:19
  52.6 13.4 %collective-permute-start.35 = (bf16[4,32,768]{2,1,0:T(8,128)(2,1)S(1)}, bf16[4,32,768]{2,1,0:T(8,128)(2,1)S(1)}, u32[]{:S(2)}, u32[]{:S(2)}) collective-permute-start(bf16[4,32,768]{2,1,0:T(8,128)(2,1)S(1)} %choose.1), channel_id=1, source_target_pairs={{0,4},{1,5},{2,6},{3,7},{4,0},{5,1},{6,2},{7,3},{8,12},{9,13},{10,... | collective-permute-start | bytes 589832 | tf_op jit(solution)/shard_map/ppermute | solution.py:19
  68.0 13.4 %collective-permute-start.45 = (bf16[8,48,384]{2,1,0:T(8,128)(2,1)S(1)}, bf16[8,48,384]{2,1,0:T(8,128)(2,1)S(1)}, u32[]{:S(2)}, u32[]{:S(2)}) collective-permute-start(bf16[8,48,384]{2,1,0:T(8,128)(2,1)S(1)} %all-to-all-done.2), channel_id=1, source_target_pairs={{0,16},{8,24},{16,0},{24,8},{1,17},{9,25},{17,1},{25,9},{2,18},{10... | collective-permute-start | bytes 884744 | tf_op jit(solution)/shard_map/ppermute | solution.py:19
  72.1 12.7 %collective-permute-start.44 = (bf16[8,48,384]{2,1,0:T(8,128)(2,1)S(1)}, bf16[8,48,384]{2,1,0:T(8,128)(2,1)S(1)}, u32[]{:S(2)}, u32[]{:S(2)}) collective-permute-start(bf16[8,48,384]{2,1,0:T(8,128)(2,1)S(1)} %all-to-all-done.2), channel_id=1, source_target_pairs={{0,8},{8,0},{16,24},{24,16},{1,9},{9,1},{17,25},{25,17},{2,10},{10... | collective-permute-start | bytes 884744 | tf_op jit(solution)/shard_map/ppermute | solution.py:19
  88.3 12.1 %collective-permute-start.48 = (bf16[4,4,16,768]{3,2,1,0:T(8,128)(2,1)S(1)}, bf16[4,4,16,768]{3,2,1,0:T(8,128)(2,1)S(1)}, u32[]{:S(2)}, u32[]{:S(2)}) collective-permute-start(bf16[4,4,16,768]{3,2,1,0:T(8,128)(2,1)S(1)} %get-tuple-element.153), channel_id=1, source_target_pairs={{0,1},{1,0},{2,3},{3,2},{4,5},{5,4},{6,7},{7,6},{8,9},{9,8},{10,11... | collective-permute-start | bytes 1179656 | tf_op jit(solution)/shard_map/ppermute | solution.py:19
  89.8 22.6 %collective-permute-start.57 = (bf16[384,768]{1,0:T(8,128)(2,1)S(1)}, bf16[384,768]{1,0:T(8,128)(2,1)S(1)}, u32[]{:S(2)}, u32[]{:S(2)}) collective-permute-start(bf16[384,768]{1,0:T(8,128)(2,1)S(1)} %grad_product.2.refs_0_), channel_id=1, source_target_pairs={{0,16},{8,24},{16,0},{24,8},{1,17},{9,25},{17,1},{25,9},{2,18},{10... | collective-permute-start | bytes 1769480 | tf_op jit(solution)/shard_map/ppermute | solution.py:19
  92.6 17.3 %collective-permute-start.43 = (bf16[8,32,384]{2,1,0:T(8,128)(2,1)S(1)}, bf16[8,32,384]{2,1,0:T(8,128)(2,1)S(1)}, u32[]{:S(2)}, u32[]{:S(2)}) collective-permute-start(bf16[8,32,384]{2,1,0:T(8,128)(2,1)S(1)} %slice_bitcast_fusion.12), channel_id=1, source_target_pairs={{0,16},{8,24},{16,0},{24,8},{1,17},{9,25},{17,1},{25,9},{2,18},{10... | collective-permute-start | bytes 589832 | tf_op jit(solution)/shard_map/ppermute | solution.py:19
  100.5 11.9 %collective-permute-start.51 = (bf16[4,16,768]{2,1,0:T(8,128)(2,1)S(1)}, bf16[4,16,768]{2,1,0:T(8,128)(2,1)S(1)}, u32[]{:S(2)}, u32[]{:S(2)}) collective-permute-start(bf16[4,16,768]{2,1,0:T(8,128)(2,1)S(1)} %get-tuple-element.213), channel_id=1, source_target_pairs={{0,6},{1,7},{2,4},{3,5},{4,2},{5,3},{6,0},{7,1},{8,14},{9,15},{10,... | collective-permute-start | bytes 294920 | tf_op jit(solution)/shard_map/ppermute | solution.py:19
  112.4 15.9 %collective-permute-start.56 = (bf16[384,768]{1,0:T(8,128)(2,1)S(1)}, bf16[384,768]{1,0:T(8,128)(2,1)S(1)}, u32[]{:S(2)}, u32[]{:S(2)}) collective-permute-start(bf16[384,768]{1,0:T(8,128)(2,1)S(1)} %grad_product.2.refs_0_), channel_id=1, source_target_pairs={{0,8},{8,0},{16,24},{24,16},{1,9},{9,1},{17,25},{25,17},{2,10},{10... | collective-permute-start | bytes 1769480 | tf_op jit(solution)/shard_map/ppermute | solution.py:19
  112.4 16.8 %collective-permute-start.58 = (bf16[384,768]{1,0:T(8,128)(2,1)S(1)}, bf16[384,768]{1,0:T(8,128)(2,1)S(1)}, u32[]{:S(2)}, u32[]{:S(2)}) collective-permute-start(bf16[384,768]{1,0:T(8,128)(2,1)S(1)} %collective-permute-done.57.refs_2_), channel_id=1, source_target_pairs={{0,8},{8,0},{16,24},{24,16},{1,9},{9,1},{17,25},{25,17},{2,10},{10... | collective-permute-start | bytes 1769480 | tf_op jit(solution)/shard_map/ppermute | solution.py:19
  113.0 13.8 %all-to-all-start.3 = ((bf16[8,32,384]{2,1,0:T(8,128)(2,1)}), bf16[8,32,384]{2,1,0:T(8,128)(2,1)S(1)}, u32[]{:S(2)}, u32[]{:S(2)}) async-start(bf16[8,32,384]{2,1,0:T(8,128)(2,1)} %fusion.4), calls=%async_computation.3 | async-start | bytes 393216 | tf_op jit(solution)/shard_map/all_to_all | solution.py:769
  142.8 14.5 %collective-permute-start.4 = (bf16[4,32,768]{2,1,0:T(8,128)(2,1)}, bf16[4,32,768]{2,1,0:T(8,128)(2,1)}, u32[]{:S(2)}, u32[]{:S(2)}) collective-permute-start(bf16[4,32,768]{2,1,0:T(8,128)(2,1)} %pad_maximum_fusion.8), channel_id=1, source_target_pairs={{0,1},{1,0},{2,3},{3,2},{4,5},{5,4},{6,7},{7,6},{8,9},{9,8},{10,11... | collective-permute-start | bytes 589832 | tf_op jit(solution)/shard_map/while/body/ppermute | solution.py:19
  143.4 15.8 %collective-permute-start.5 = (bf16[4,32,768]{2,1,0:T(8,128)(2,1)}, bf16[4,32,768]{2,1,0:T(8,128)(2,1)}, u32[]{:S(2)}, u32[]{:S(2)}) collective-permute-start(bf16[4,32,768]{2,1,0:T(8,128)(2,1)} %pad_maximum_fusion.8), channel_id=1, source_target_pairs={{0,2},{1,3},{2,0},{3,1},{4,6},{5,7},{6,4},{7,5},{8,10},{9,11},{10,... | collective-permute-start | bytes 589832 | tf_op jit(solution)/shard_map/while/body/ppermute | solution.py:19
  146.1 33.9 %collective-permute-start.10 = (bf16[384,768]{1,0:T(8,128)(2,1)}, bf16[384,768]{1,0:T(8,128)(2,1)S(1)}, u32[]{:S(2)}, u32[]{:S(2)}) collective-permute-start(bf16[384,768]{1,0:T(8,128)(2,1)} %get-tuple-element.349), channel_id=1, source_target_pairs={{0,16},{8,24},{16,0},{24,8},{1,17},{9,25},{17,1},{25,9},{2,18},{10... | collective-permute-start | bytes 1769480 | tf_op jit(solution)/shard_map/while/body/ppermute | solution.py:19
  147.3 40.1 %collective-permute-start.16 = (bf16[384,768]{1,0:T(8,128)(2,1)}, bf16[384,768]{1,0:T(8,128)(2,1)S(1)}, u32[]{:S(2)}, u32[]{:S(2)}) collective-permute-start(bf16[384,768]{1,0:T(8,128)(2,1)} %get-tuple-element.354), channel_id=1, source_target_pairs={{0,16},{8,24},{16,0},{24,8},{1,17},{9,25},{17,1},{25,9},{2,18},{10... | collective-permute-start | bytes 1769480 | tf_op jit(solution)/shard_map/while/body/ppermute | solution.py:19
  149.7 12.4 %collective-permute-start.7 = (bf16[4,32,768]{2,1,0:T(8,128)(2,1)}, bf16[4,32,768]{2,1,0:T(8,128)(2,1)}, u32[]{:S(2)}, u32[]{:S(2)}) collective-permute-start(bf16[4,32,768]{2,1,0:T(8,128)(2,1)} %pad_maximum_fusion.8), channel_id=1, source_target_pairs={{0,4},{1,5},{2,6},{3,7},{4,0},{5,1},{6,2},{7,3},{8,12},{9,13},{10,... | collective-permute-start | bytes 589832 | tf_op jit(solution)/shard_map/while/body/ppermute | solution.py:19
  153.2 19.0 %all-to-all-start.1 = ((bf16[8,48,384]{2,1,0:T(8,128)(2,1)}), bf16[8,48,384]{2,1,0:T(8,128)(2,1)}, u32[]{:S(2)}, u32[]{:S(2)}) async-start(bf16[8,48,384]{2,1,0:T(8,128)(2,1)} %features.3), calls=%async_computation.1 | async-start | bytes 589824 | tf_op jit(solution)/shard_map/while/body/all_to_all | solution.py:747
  157.4 22.6 %collective-permute-start.9 = (bf16[4,32,768]{2,1,0:T(8,128)(2,1)}, bf16[4,32,768]{2,1,0:T(8,128)(2,1)S(1)}, u32[]{:S(2)}, u32[]{:S(2)}) collective-permute-start(bf16[4,32,768]{2,1,0:T(8,128)(2,1)} %copy-done.30), channel_id=1, source_target_pairs={{0,1},{1,0},{2,3},{3,2},{4,5},{5,4},{6,7},{7,6},{8,9},{9,8},{10,11... | collective-permute-start | bytes 589832 | tf_op jit(solution)/shard_map/while/body/ppermute | solution.py:19
  159.3 12.0 %collective-permute-start.6 = (bf16[4,32,768]{2,1,0:T(8,128)(2,1)}, bf16[4,32,768]{2,1,0:T(8,128)(2,1)S(1)}, u32[]{:S(2)}, u32[]{:S(2)}) collective-permute-start(bf16[4,32,768]{2,1,0:T(8,128)(2,1)} %collective-permute-done.5), channel_id=1, source_target_pairs={{0,1},{1,0},{2,3},{3,2},{4,5},{5,4},{6,7},{7,6},{8,9},{9,8},{10,11... | collective-permute-start | bytes 589832 | tf_op jit(solution)/shard_map/while/body/ppermute | solution.py:19
  162.1 13.0 %collective-permute-start.8 = (bf16[4,32,768]{2,1,0:T(8,128)(2,1)}, bf16[4,32,768]{2,1,0:T(8,128)(2,1)}, u32[]{:S(2)}, u32[]{:S(2)}) collective-permute-start(bf16[4,32,768]{2,1,0:T(8,128)(2,1)} %collective-permute-done.7), channel_id=1, source_target_pairs={{0,1},{1,0},{2,3},{3,2},{4,5},{5,4},{6,7},{7,6},{8,9},{9,8},{10,11... | collective-permute-start | bytes 589832 | tf_op jit(solution)/shard_map/while/body/ppermute | solution.py:19
  185.2 32.1 %collective-permute-start.24 = (bf16[64,3072]{1,0:T(8,128)(2,1)}, bf16[64,3072]{1,0:T(8,128)(2,1)S(1)}, u32[]{:S(2)}, u32[]{:S(2)}) collective-permute-start(bf16[64,3072]{1,0:T(8,128)(2,1)} %send_blocks.11), channel_id=1, source_target_pairs={{0,16},{8,24},{16,0},{24,8},{1,17},{9,25},{17,1},{25,9},{2,18},{10... | collective-permute-start | bytes 1179656 | tf_op jit(solution)/shard_map/while/body/ppermute | solution.py:19
  189.8 13.3 %collective-permute-start.12 = (bf16[8,32,384]{2,1,0:T(8,128)(2,1)S(1)}, bf16[8,32,384]{2,1,0:T(8,128)(2,1)S(1)}, u32[]{:S(2)}, u32[]{:S(2)}) collective-permute-start(bf16[8,32,384]{2,1,0:T(8,128)(2,1)S(1)} %slice_bitcast_fusion.23), channel_id=1, source_target_pairs={{0,16},{8,24},{16,0},{24,8},{1,17},{9,25},{17,1},{25,9},{2,18},{10... | collective-permute-start | bytes 589832 | tf_op jit(solution)/shard_map/while/body/ppermute | solution.py:19
  192.8 20.6 %collective-permute-start.26 = (bf16[384,768]{1,0:T(8,128)(2,1)S(1)}, bf16[384,768]{1,0:T(8,128)(2,1)S(1)}, u32[]{:S(2)}, u32[]{:S(2)}) collective-permute-start(bf16[384,768]{1,0:T(8,128)(2,1)S(1)} %grad_product.3.refs_0_), channel_id=1, source_target_pairs={{0,16},{8,24},{16,0},{24,8},{1,17},{9,25},{17,1},{25,9},{2,18},{10... | collective-permute-start | bytes 1769480 | tf_op jit(solution)/shard_map/while/body/ppermute | solution.py:19
  209.7 16.0 %collective-permute-start.25 = (bf16[384,768]{1,0:T(8,128)(2,1)S(1)}, bf16[384,768]{1,0:T(8,128)(2,1)S(1)}, u32[]{:S(2)}, u32[]{:S(2)}) collective-permute-start(bf16[384,768]{1,0:T(8,128)(2,1)S(1)} %grad_product.3.refs_0_), channel_id=1, source_target_pairs={{0,8},{8,0},{16,24},{24,16},{1,9},{9,1},{17,25},{25,17},{2,10},{10... | collective-permute-start | bytes 1769480 | tf_op jit(solution)/shard_map/while/body/ppermute | solution.py:19
  213.4 12.3 %collective-permute-start.27 = (bf16[384,768]{1,0:T(8,128)(2,1)S(1)}, bf16[384,768]{1,0:T(8,128)(2,1)S(1)}, u32[]{:S(2)}, u32[]{:S(2)}) collective-permute-start(bf16[384,768]{1,0:T(8,128)(2,1)S(1)} %collective-permute-done.26.refs_2_), channel_id=1, source_target_pairs={{0,8},{8,0},{16,24},{24,16},{1,9},{9,1},{17,25},{25,17},{2,10},{10... | collective-permute-start | bytes 1769480 | tf_op jit(solution)/shard_map/while/body/ppermute | solution.py:19
  231.7 14.2 %collective-permute-start.61 = (bf16[48,3072]{1,0:T(8,128)(2,1)S(1)}, bf16[48,3072]{1,0:T(8,128)(2,1)S(1)}, u32[]{:S(2)}, u32[]{:S(2)}) collective-permute-start(bf16[48,3072]{1,0:T(8,128)(2,1)S(1)} %get-tuple-element.164), channel_id=1, source_target_pairs={{0,24},{8,16},{16,8},{24,0},{1,25},{9,17},{17,9},{25,1},{2,26},{10... | collective-permute-start | bytes 884744 | tf_op jit(solution)/shard_map/ppermute | solution.py:19
  (75 other events, 530.6 us)
